TPU v7x, 32 devices: a whole 2x2x4 slice. The times are simulated.
32 devices in a mesh: rad: 2 (over x), chan: 16 (over z, y, core).
Axes of the slice: x: 2, y: 2, z: 4, core: 2. Of those that a mesh axis runs over, the one named last changes fastest.
Arguments:
- wave: float32 [512, 8, 4096], P('chan', 'rad'), may hold values from -9 to 9
- coupling: float32 [3, 512, 512], replicated, may hold values from -32 to 32
- channels: int32 [512, 3], replicated, may hold values from 0 to 3
Outputs:
- wave_out: float32 [512, 8, 4096], P('chan', 'rad')
Inputs may be any that keep to these rules, and one draw needn't show every extreme that they name: `channels`: each column holds an angular momentum number.
All inputs are finite; a program needn't handle non-finite values.
Results may differ from a plain program's by a relative error of at most 0.0003.
Values sent between devices are 32-bit elements; how exact they have to be, the bound alone decides.
No kernel may reach another device: no remote copies, remote signals or barrier semaphores. Data moves between devices by JAX's collectives and lax.ppermute only.
A program may use at most 448 MiB of HBM per device.

v0:
```python
import jax
import jax.numpy as jnp
from jax import lax
from jax.sharding import PartitionSpec as P

step_h = 0.25
step_tau = 0.02
row_start = 2.0
box_first = 8.0


def with_halo(shard, sides, width):
    for axis, dim in sides:
        devices, length = (lax.axis_size(axis), shard.shape[dim])
        up = [(i, (i + 1) % devices) for i in range(devices - 1)]
        down = [(j, i) for i, j in up]
        last = lax.slice_in_dim(shard, length - width, length, axis=dim)
        initial = lax.slice_in_dim(shard, 0, width, axis=dim)
        before = lax.ppermute(last, axis, up)
        after = lax.ppermute(initial, axis, down)
        shard = jnp.concatenate([before, shard, after], axis=dim)
    return shard


def potential(lvalue, radius):
    return -2.0 / radius + lvalue * (lvalue + 1.0) / (2.0 * radius * radius)


def row_update(padded, centre, pot):
    lap = padded[:, 2:, :] + padded[:, :-2, :] - 2.0 * centre
    return centre - step_tau * (-0.5 / (step_h * step_h) * lap + pot * centre)


def crank_source(field, pot, first_h):
    padded = jnp.pad(field, ((0, 0), (0, 0), (1, 1)))
    lap = padded[:, :, 2:] + padded[:, :, :-2] - 2.0 * field
    hfield = -0.5 / (first_h * first_h) * lap + pot[:, None, :] * field
    return field - 0.5 * step_tau * hfield


def interface_marks(block_count, tile_width):
    place = jnp.arange(tile_width)[None, :]
    which = jnp.arange(block_count)[:, None]
    first_mark = (place == 0) & (which >= 1)
    last_mark = (place == tile_width - 1) & (which <= block_count - 2)
    return (first_mark, last_mark)


def solve_tables(pot, first_h):
    nchan = pot.shape[0]
    length = pot.shape[1]
    tile_width = 128
    block_count = length // tile_width
    coeff = 1.0 / (first_h * first_h)
    offval = -step_tau * 0.25 * coeff
    diagonal = (1.0 + 0.5 * step_tau * (coeff + pot)).reshape(nchan, block_count, tile_width)
    first_mark, last_mark = interface_marks(block_count, tile_width)
    marked = first_mark | last_mark
    false_column = jnp.zeros((block_count, 1), dtype=bool)
    before = jnp.concatenate([false_column, marked[:, :-1]], axis=1)
    after = jnp.concatenate([marked[:, 1:], false_column], axis=1)
    place = jnp.arange(tile_width)[None, :]
    keep_below = (place > 0) & jnp.logical_not(marked) & jnp.logical_not(before)
    keep_above = (place < tile_width - 1) & jnp.logical_not(marked) & jnp.logical_not(after)
    below = jnp.broadcast_to(jnp.where(keep_below, offval, 0.0), diagonal.shape).astype(
        diagonal.dtype
    )
    above = jnp.broadcast_to(jnp.where(keep_above, offval, 0.0), diagonal.shape).astype(
        diagonal.dtype
    )
    centre = jnp.where(marked[None], 1.0, diagonal)
    unit = jnp.broadcast_to(
        jnp.eye(tile_width, dtype=diagonal.dtype), (nchan, block_count, tile_width, tile_width)
    )
    inverse = lax.linalg.tridiagonal_solve(below, centre, above, unit)
    square = offval * offval
    which = jnp.arange(block_count)
    has_first = which >= 1
    has_last = which <= block_count - 2
    schur_first = jnp.where(has_first, diagonal[:, :, 0] - square * inverse[:, :, 1, 1], 1.0)
    schur_last = jnp.where(
        has_last,
        diagonal[:, :, tile_width - 1] - square * inverse[:, :, tile_width - 2, tile_width - 2],
        1.0,
    )
    inside = jnp.where(has_first & has_last, -square * inverse[:, :, 1, tile_width - 2], 0.0)
    across = jnp.broadcast_to(jnp.where(has_last, offval, 0.0), inside.shape).astype(diagonal.dtype)
    order = 2 * block_count
    schur_centre = (
        jnp.stack([schur_first, schur_last], axis=-1).reshape(nchan, order).astype(diagonal.dtype)
    )
    coupling_next = (
        jnp.stack([inside, across], axis=-1).reshape(nchan, order).astype(diagonal.dtype)
    )
    coupling_prev = jnp.concatenate(
        [jnp.zeros((nchan, 1), diagonal.dtype), coupling_next[:, :-1]], axis=1
    )
    schur_unit = jnp.broadcast_to(jnp.eye(order, dtype=diagonal.dtype), (nchan, order, order))
    schur_inverse = lax.linalg.tridiagonal_solve(
        coupling_prev, schur_centre, coupling_next, schur_unit
    )
    return (inverse, schur_inverse, offval)


def blocked_solve(source, inverse, schur_inverse, offval):
    nchan = source.shape[0]
    rows = source.shape[1]
    length = source.shape[2]
    tile_width = inverse.shape[-1]
    block_count = length // tile_width
    first_mark, last_mark = interface_marks(block_count, tile_width)
    marked = first_mark | last_mark
    pieces = source.reshape(nchan, rows, block_count, tile_width)
    interior = jnp.where(marked, 0.0, pieces)
    block_part = jnp.einsum("cbik,crbk->crbi", inverse, interior, precision=lax.Precision.HIGHEST)
    which = jnp.arange(block_count)
    source_first = jnp.where(which >= 1, pieces[..., 0] - offval * block_part[..., 1], 0.0)
    source_last = jnp.where(
        which <= block_count - 2,
        pieces[..., tile_width - 1] - offval * block_part[..., tile_width - 2],
        0.0,
    )
    sources = jnp.stack([source_first, source_last], axis=-1).reshape(nchan, rows, 2 * block_count)
    ends = jnp.einsum("cmn,crn->crm", schur_inverse, sources, precision=lax.Precision.HIGHEST)
    ends = ends.reshape(nchan, rows, block_count, 2)
    end_first = ends[..., 0]
    end_last = ends[..., 1]
    column_first = inverse[:, :, :, 1]
    column_last = inverse[:, :, :, tile_width - 2]
    solved = block_part - offval * (
        column_first[:, None] * end_first[..., None] + column_last[:, None] * end_last[..., None]
    )
    solved = (
        solved
        + jnp.where(first_mark, end_first[..., None], 0.0)
        + jnp.where(last_mark, end_last[..., None], 0.0)
    )
    return solved.reshape(nchan, rows, length)


def radial_factors(rfirst, rsecond):
    rmin = jnp.minimum(rsecond[:, None], rfirst[None, :])
    rmax = jnp.maximum(rsecond[:, None], rfirst[None, :])
    return jnp.stack([1.0 / rmax, rmin / (rmax * rmax), rmin * rmin / (rmax * rmax * rmax)])


def apply_repulsion(flat, mats, factors):
    total = factors[0] * jnp.dot(mats[0], flat, precision=lax.Precision.HIGHEST)
    total = total + factors[1] * jnp.dot(mats[1], flat, precision=lax.Precision.HIGHEST)
    total = total + factors[2] * jnp.dot(mats[2], flat, precision=lax.Precision.HIGHEST)
    return total


def taylor_repel(flat, mats, factors):
    first = apply_repulsion(flat, mats, factors)
    second = apply_repulsion(first, mats, factors)
    third = apply_repulsion(second, mats, factors)
    return (
        flat
        - step_tau * first
        + step_tau * step_tau / 2.0 * second
        - step_tau * step_tau * step_tau / 6.0 * third
    )


def multipole_mats(coupling, channels):
    same = (channels[:, 2][:, None] == channels[None, :, 2]).astype(coupling.dtype)
    return 0.5 * (coupling + jnp.transpose(coupling, (0, 2, 1))) * same[None]


def rows_with_rim(field, pot_rows):
    padded = with_halo(field, (("rad", 1),), 1)
    return row_update(padded, field, pot_rows)


def on_device(wave, coupling, channels):
    nchan_dev = wave.shape[0]
    rows = wave.shape[1]
    length = wave.shape[2]
    total_chan = channels.shape[0]
    chan_count = lax.axis_size("chan")
    chan_index = lax.axis_index("chan")
    rad_index = lax.axis_index("rad")
    first_h = box_first / length
    mats = multipole_mats(coupling, channels)
    lfirst_all = channels[:, 0].astype(jnp.float32)
    lsecond_all = channels[:, 1].astype(jnp.float32)
    lfirst = lax.dynamic_slice_in_dim(lfirst_all, chan_index * nchan_dev, nchan_dev)
    lsecond = lax.dynamic_slice_in_dim(lsecond_all, chan_index * nchan_dev, nchan_dev)
    rfirst = (jnp.arange(length) + 1).astype(jnp.float32) * first_h
    rsecond = (rad_index * rows + jnp.arange(rows) + 1).astype(jnp.float32) * step_h + row_start
    pot_first = potential(lfirst[:, None], rfirst[None, :])
    pot_second = potential(lsecond[:, None], rsecond[None, :])[:, :, None]
    inverse, schur_inverse, offval = solve_tables(pot_first, first_h)
    block = length // chan_count
    point_first = (chan_index * block + jnp.arange(block) + 1).astype(jnp.float32) * first_h
    factors = radial_factors(point_first, rsecond).reshape(3, rows * block)
    psi = wave
    psi = rows_with_rim(psi, pot_second)
    psi = blocked_solve(crank_source(psi, pot_first, first_h), inverse, schur_inverse, offval)
    points = lax.all_to_all(psi, "chan", split_axis=2, concat_axis=0, tiled=True)
    flat = taylor_repel(points.reshape(total_chan, rows * block), mats, factors)
    points = flat.reshape(total_chan, rows, block)
    psi = lax.all_to_all(points, "chan", split_axis=0, concat_axis=2, tiled=True)
    return psi


def solution(mesh):
    in_specs = (P("chan", "rad", None), P(), P())
    out_specs = P("chan", "rad", None)
    return jax.shard_map(
        on_device, mesh=mesh, in_specs=in_specs, out_specs=out_specs, check_vma=False
    )
```

profile of v0, /device:TPU:9, one launch (start us, length us, event | category | flops | bytes accessed | tf_op | source)
XLA Modules:
  0.0 1463.8 jit_solution(13988627132920576221)
XLA Ops:
  6.9 5.6 collective-permute-start.1
  27.7 16.4 %transpose.819 = f32[3,32,32,32,128]{4,3,2,1,0:T(8,128)} broadcast(f32[3,32,128]{2,1,0:T(8,128)S(1)} %bitcast.4629), dimensions={0,1,4} | broadcast | bytes 50380800 | tf_op jit(solution)/shard_map/vmap(vmap())/transpose | solution.py:75
  44.1 345.4 %while.8 = (s32[]{:T(128)}, f32[32,32]{1,0:T(8,128)S(1)}, f32[32,32,128]{2,1,0:T(8,128)S(1)}, f32[3,32,32,32]{3,2,1,0:T(8,128)}, f32[3,32,32,32,128]{4,3,2,1,0:T...) while((s32[]{:T(128)}, f32[32,32]{1,0:T(8,128)S(1)}, ...), condition=%wide.region_1.2_spmd, body=%wide.region_0.1_spmd.sunk | while | flops 19004448 | bytes 105461576 | solution.py:75
  144.2 11.7 bitcast_dynamic-update-slice_fusion.196
  259.1 11.7 bitcast_dynamic-update-slice_fusion.196
  374.0 11.6 bitcast_dynamic-update-slice_fusion.196
  391.7 5.7 slice_reduce_fusion.30
  460.3 10.5 concatenate.66
  473.6 34.4 %constant_dynamic-update-slice_fusion.32 = f32[127,32,32,128]{3,2,1,0:T(8,128)} fusion(f32[96,32,32,128]{3,2,1,0:T(8,128)} %bitcast.4571), kind=kLoop, calls=%fused_computation.799 | loop fusion | bytes 100663296
  584.6 34.2 %slice.4338 = f32[96,32,32,128]{3,2,1,0:T(8,128)} slice(f32[127,32,32,128]{3,2,1,0:T(8,128)} %bitcast_dynamic-update-slice_fusion.66), slice={[31:127], [0:32], [0:32], [0:128]} | slice | bytes 100663296 | tf_op jit(solution)/shard_map/vmap(vmap())/slice | solution.py:75
  620.9 16.5 %broadcast.110831.clone = f32[3,32,32,32,128]{4,1,0,3,2:T(8,128)} broadcast(f32[]{:T(128)} %constant.138.clone.1), dimensions={} | broadcast | bytes 50331652 | tf_op jit(solution)/shard_map/broadcast.23
  637.6 129.3 %while.9 = (s32[]{:T(128)}, f32[32,32,128]{2,1,0:T(8,128)S(1)}, f32[3,32,32,32,128]{4,1,0,3,2:T(8,128)}, f32[3,32,32,32,128]{4,3,2,1,0:T(8,128)}, f32[3,32,32,32...) while((s32[]{:T(128)}, f32[32,32,128]{2,1,0:T(8,128)S(1)}, ...), condition=%wide.region_3.4_spmd, body=%wide.region_2.3_spmd.sunk | while | flops 12582945 | bytes 101831760 | solution.py:75
  638.2 7.7 bitcast_dynamic-update-slice_fusion.197
  665.5 14.0 copy_dynamic-update-slice_fusion.2
  681.2 7.7 bitcast_dynamic-update-slice_fusion.197
  708.4 14.0 copy_dynamic-update-slice_fusion.2
  724.2 7.7 bitcast_dynamic-update-slice_fusion.197
  751.5 13.9 copy_dynamic-update-slice_fusion.2
  767.1 11.7 fusion.352
  778.8 194.9 %concatenate.67 = f32[127,32,32,128]{3,0,2,1:T(8,128)} concatenate(f32[1,32,32,128]{3,0,2,1:T(1,128)S(1)} %bitcast.4590, f32[1,32,32,128]{3,0,2,1:T(1,128)S(1)} %bitcast.4591, f32[1,32,32,128]{3,0,2,1:T(1,128)S(1)} %bitcast.4592, f32[1,32,32,128]{3,0,2,1:T(1,128)S(1)} %bitcast.4593, f32[1,32,32,128]{3,0,2,1:T(1,128)} %bitcast.4594, f32[1,32,32,128]{3,0,2,1:T(1,128)} %bitcast.4595, ...), dimensions={0} | concatenate | bytes 133169152 | tf_op jit(solution)/shard_map/vmap(vmap())/concatenate | solution.py:75
  973.7 30.7 %fusion.353 = (f32[32,32]{1,0:T(8,128)S(1)}, f32[32,32]{1,0:T(8,128)S(1)}, f32[32,32]{1,0:T(8,128)S(1)}) fusion(f32[32,32,127,128]{3,2,1,0:T(8,128)} %bitcast.587), kind=kLoop, calls=%fused_computation.795 | loop fusion | flops 3072 | bytes 24576 | tf_op jit(solution)/shard_map/mul | solution.py:80
  1011.9 80.5 %fusion.290 = (f32[32,32,128]{2,1,0:T(8,128)}, f32[32,32,128]{2,1,0:T(8,128)}) fusion(f32[32,32,1,128]{3,2,1,0:T(1,128)S(1)} %bitcast.4587, f32[32,32,127,128]{3,2,1,0:T(8,128)} %bitcast.587), kind=kLoop, calls=%fused_computation.584 | loop fusion | flops 262144 | bytes 68157440 | tf_op jit(solution)/shard_map/slice | solution.py:128
  1144.2 108.1 %fusion.309 = f32[32,4,32,128]{3,1,2,0:T(4,128)S(1)} fusion(f32[32,32,1,128]{3,2,1,0:T(1,128)S(1)} %bitcast.4588, f32[32,32,127,128]{3,2,1,0:T(8,128)} %bitcast.587, f32[32,4,32,128]{3,1,2,0:T(4,128)S(1)} %subtract_bitcast_fusion, pred[32,128]{1,0:T(8,128)(4,1)S(1)} %copy.514), kind=kOutput, calls=%fused_computation.617 | convolution fusion | flops 822607872 | bytes 71307264 | tf_op jit(solution)/shard_map/cbik,crbk->crbi/dot_general | solution.py:115
  1264.7 6.9 select_add_fusion
  1271.6 8.0 copy.604
  1279.6 9.5 reshape.192760
  1289.1 7.2 all-to-all-start
  1302.7 39.7 %all-to-all-done = f32[16,1,32768]{2,1,0:T(1,128)} async-done(((f32[16,1,32768]{2,1,0:T(1,128)}), f32[16,1,32768]{2,1,0:T(1,128)}, u32[]{:S(2)}, u32[]{:S(2)}) %all-to-all-start) | async-done | bytes 2097184 | tf_op jit(solution)/shard_map/all_to_all | solution.py:201
  1342.9 8.5 reduce.72
  1351.4 7.7 reshape.192761
  1359.1 6.4 copy.605
  1406.1 54.0 %all_to_all.33 = f32[512,4,256]{2,1,0:T(4,128)S(1)} all-to-all(f32[512,4,256]{2,1,0:T(4,128)S(1)} %reshape.192723), channel_id=1, replica_groups=mesh['rad'=2,'chan'=16] {'chan'}, dimensions={0} | all-to-all | bytes 4194304 | tf_op jit(solution)/shard_map/all_to_all | solution.py:204
  (856 shorter events, 661.9 us)
Async XLA Ops:
  4.5 1131.3 %collective-permute-start = (f32[32,1,4096]{2,0,1:T(8,128)}, f32[32,1,4096]{2,0,1:T(8,128)}, u32[]{:S(2)}, u32[]{:S(2)}) collective-permute-start(f32[32,1,4096]{2,0,1:T(8,128)} %copy.609), channel_id=1, source_target_pairs={{16,0},{17,1},{18,2},{19,3},{20,4},{21,5},{22,6},{23,7},{24,8},{25... | collective-permute-start | bytes 1572872 | tf_op jit(solution)/shard_map/ppermute | solution.py:20
  6.9 1130.5 %collective-permute-start.1 = (f32[32,1,4096]{2,0,1:T(8,128)}, f32[32,1,4096]{2,0,1:T(8,128)}, u32[]{:S(2)}, u32[]{:S(2)}) collective-permute-start(f32[32,1,4096]{2,0,1:T(8,128)} %copy.610), channel_id=1, source_target_pairs={{0,16},{1,17},{2,18},{3,19},{4,20},{5,21},{6,22},{7,23},{8,24},{9,... | collective-permute-start | bytes 1572872 | tf_op jit(solution)/shard_map/ppermute | solution.py:19
  637.4 129.5 %copy-start.43 = (f32[32,32]{1,0:T(8,128)S(1)}, f32[32,32]{1,0:T(8,128)}, u32[]{:S(2)}) copy-start(f32[32,32]{1,0:T(8,128)} %get-tuple-element.232) | copy-start | bytes 12292
  637.4 129.5 %copy-start.44 = (f32[32,32]{1,0:T(8,128)S(1)}, f32[32,32]{1,0:T(8,128)}, u32[]{:S(2)}) copy-start(f32[32,32]{1,0:T(8,128)} %get-tuple-element.233) | copy-start | bytes 12292
  637.4 129.5 %copy-start.45 = (f32[32,32]{1,0:T(8,128)S(1)}, f32[32,32]{1,0:T(8,128)}, u32[]{:S(2)}) copy-start(f32[32,32]{1,0:T(8,128)} %get-tuple-element.234) | copy-start | bytes 12292
  637.4 129.5 %copy-start.46 = (f32[32,32]{1,0:T(8,128)S(1)}, f32[32,32]{1,0:T(8,128)}, u32[]{:S(2)}) copy-start(f32[32,32]{1,0:T(8,128)} %get-tuple-element.235) | copy-start | bytes 12292
  637.4 129.5 %copy-start.47 = (f32[32,32]{1,0:T(8,128)S(1)}, f32[32,32]{1,0:T(8,128)}, u32[]{:S(2)}) copy-start(f32[32,32]{1,0:T(8,128)} %get-tuple-element.236) | copy-start | bytes 12292
  637.4 129.5 %copy-start.48 = (f32[32,32]{1,0:T(8,128)S(1)}, f32[32,32]{1,0:T(8,128)}, u32[]{:S(2)}) copy-start(f32[32,32]{1,0:T(8,128)} %get-tuple-element.237) | copy-start | bytes 12292
  637.4 129.5 %copy-start.49 = (f32[32,32]{1,0:T(8,128)S(1)}, f32[32,32]{1,0:T(8,128)}, u32[]{:S(2)}) copy-start(f32[32,32]{1,0:T(8,128)} %get-tuple-element.238) | copy-start | bytes 12292
  637.4 129.5 %copy-start.50 = (f32[32,32]{1,0:T(8,128)S(1)}, f32[32,32]{1,0:T(8,128)}, u32[]{:S(2)}) copy-start(f32[32,32]{1,0:T(8,128)} %get-tuple-element.239) | copy-start | bytes 12292
  637.4 129.5 %copy-start.51 = (f32[32,32]{1,0:T(8,128)S(1)}, f32[32,32]{1,0:T(8,128)}, u32[]{:S(2)}) copy-start(f32[32,32]{1,0:T(8,128)} %get-tuple-element.240) | copy-start | bytes 12292
  637.5 129.5 %copy-start.52 = (f32[32,32]{1,0:T(8,128)S(1)}, f32[32,32]{1,0:T(8,128)}, u32[]{:S(2)}) copy-start(f32[32,32]{1,0:T(8,128)} %get-tuple-element.241) | copy-start | bytes 12292
  637.5 129.5 %copy-start.53 = (f32[32,32]{1,0:T(8,128)S(1)}, f32[32,32]{1,0:T(8,128)}, u32[]{:S(2)}) copy-start(f32[32,32]{1,0:T(8,128)} %get-tuple-element.242) | copy-start | bytes 12292
  637.5 129.5 %copy-start.54 = (f32[32,32]{1,0:T(8,128)S(1)}, f32[32,32]{1,0:T(8,128)}, u32[]{:S(2)}) copy-start(f32[32,32]{1,0:T(8,128)} %get-tuple-element.243) | copy-start | bytes 12292
  637.5 129.5 %copy-start.55 = (f32[32,32]{1,0:T(8,128)S(1)}, f32[32,32]{1,0:T(8,128)}, u32[]{:S(2)}) copy-start(f32[32,32]{1,0:T(8,128)} %get-tuple-element.244) | copy-start | bytes 12292
  637.5 129.5 %copy-start.56 = (f32[32,32]{1,0:T(8,128)S(1)}, f32[32,32]{1,0:T(8,128)}, u32[]{:S(2)}) copy-start(f32[32,32]{1,0:T(8,128)} %get-tuple-element.245) | copy-start | bytes 12292
  637.5 129.5 %copy-start.57 = (f32[32,32]{1,0:T(8,128)S(1)}, f32[32,32]{1,0:T(8,128)}, u32[]{:S(2)}) copy-start(f32[32,32]{1,0:T(8,128)} %get-tuple-element.246) | copy-start | bytes 12292
  637.5 129.5 %copy-start.58 = (f32[32,32]{1,0:T(8,128)S(1)}, f32[32,32]{1,0:T(8,128)}, u32[]{:S(2)}) copy-start(f32[32,32]{1,0:T(8,128)} %get-tuple-element.247) | copy-start | bytes 12292
  637.5 129.5 %copy-start.59 = (f32[32,32]{1,0:T(8,128)S(1)}, f32[32,32]{1,0:T(8,128)}, u32[]{:S(2)}) copy-start(f32[32,32]{1,0:T(8,128)} %get-tuple-element.248) | copy-start | bytes 12292
  637.5 129.5 %copy-start.60 = (f32[32,32]{1,0:T(8,128)S(1)}, f32[32,32]{1,0:T(8,128)}, u32[]{:S(2)}) copy-start(f32[32,32]{1,0:T(8,128)} %get-tuple-element.249) | copy-start | bytes 12292
  637.5 129.5 %copy-start.61 = (f32[32,32]{1,0:T(8,128)S(1)}, f32[32,32]{1,0:T(8,128)}, u32[]{:S(2)}) copy-start(f32[32,32]{1,0:T(8,128)} %get-tuple-element.250) | copy-start | bytes 12292
  637.6 129.5 %copy-start.62 = (f32[32,32]{1,0:T(8,128)S(1)}, f32[32,32]{1,0:T(8,128)}, u32[]{:S(2)}) copy-start(f32[32,32]{1,0:T(8,128)} %get-tuple-element.251) | copy-start | bytes 12292
  637.6 129.5 %copy-start.63 = (f32[32,32]{1,0:T(8,128)S(1)}, f32[32,32]{1,0:T(8,128)}, u32[]{:S(2)}) copy-start(f32[32,32]{1,0:T(8,128)} %get-tuple-element.252) | copy-start | bytes 12292
  637.6 129.5 %copy-start.64 = (f32[32,32]{1,0:T(8,128)S(1)}, f32[32,32]{1,0:T(8,128)}, u32[]{:S(2)}) copy-start(f32[32,32]{1,0:T(8,128)} %get-tuple-element.253) | copy-start | bytes 12292
  637.6 129.5 %copy-start.65 = (f32[32,32]{1,0:T(8,128)S(1)}, f32[32,32]{1,0:T(8,128)}, u32[]{:S(2)}) copy-start(f32[32,32]{1,0:T(8,128)} %get-tuple-element.254) | copy-start | bytes 12292
  637.6 129.5 %copy-start.66 = (f32[32,32]{1,0:T(8,128)S(1)}, f32[32,32]{1,0:T(8,128)}, u32[]{:S(2)}) copy-start(f32[32,32]{1,0:T(8,128)} %get-tuple-element.255) | copy-start | bytes 12292
  637.6 129.5 %copy-start.67 = (f32[32,32]{1,0:T(8,128)S(1)}, f32[32,32]{1,0:T(8,128)}, u32[]{:S(2)}) copy-start(f32[32,32]{1,0:T(8,128)} %get-tuple-element.256) | copy-start | bytes 12292
  778.8 225.6 %copy-start.134 = (pred[32]{0:T(512)(128)(4,1)S(1)}, pred[32]{0:T(512)(128)(4,1)}, u32[]{:S(2)}) copy-start(pred[32]{0:T(512)(128)(4,1)} %copy-done.133) | copy-start | bytes 100
  778.8 225.6 %copy-start.137 = (pred[32]{0:T(512)(128)(4,1)S(1)}, pred[32]{0:T(512)(128)(4,1)}, u32[]{:S(2)}) copy-start(pred[32]{0:T(512)(128)(4,1)} %copy-done.136) | copy-start | bytes 100
  778.8 226.5 %copy-start.148 = (pred[32]{0:T(512)(128)(4,1)S(1)}, pred[32]{0:T(512)(128)(4,1)}, u32[]{:S(2)}) copy-start(pred[32]{0:T(512)(128)(4,1)} %fusion.559) | copy-start | bytes 100
  778.8 226.5 %copy-start.149 = (f32[32]{0:T(128)S(1)}, f32[32]{0:T(128)}, u32[]{:S(2)}) copy-start(f32[32]{0:T(128)} %broadcast_select_fusion.1) | copy-start | bytes 388
  1289.1 53.3 %all-to-all-start = ((f32[16,1,32768]{2,1,0:T(1,128)}), f32[16,1,32768]{2,1,0:T(1,128)}, u32[]{:S(2)}, u32[]{:S(2)}) async-start(f32[16,1,32768]{2,1,0:T(1,128)} %reshape.192760), calls=%async_computation | async-start | bytes 4194304 | tf_op jit(solution)/shard_map/all_to_all | solution.py:201
  (122 other events, 7190.8 us)
where the time goes:
time: 1490 us; the launch traced here: 1460 us
  other arithmetic  673 us (45%)
  local copies, waits for them, and re-layouts  533 us (36%)
  matrix products  145 us (10%)
  blocking collectives  54 us (4%)
  waiting for transfers between devices  39.7 us (3%)
    while x228, other arithmetic  364 us
    concatenate x5, local copies, waits for them, and re-layouts, solve_tables(): inverse = lax.linalg.tridiagonal_solve(below, centre, above, unit)  205 us
    dot_general x1, matrix products, blocked_solve(): jnp.einsum('cbik,crbk->crbi', inverse, interior, precision=lax.Precision....  108 us
    unnamed x83, other arithmetic  104 us
    slice x1, other arithmetic, blocked_solve(): column_first = inverse[:, :, :, 1]  80.5 us
    dynamic_update_slice x9, local copies, waits for them, and re-layouts, solve_tables(): inverse = lax.linalg.tridiagonal_solve(below, centre, above, unit)  79.4 us
    unnamed x320, local copies, waits for them, and re-layouts  59.4 us
    all_to_all x1, blocking collectives, on_device(): lax.all_to_all(points, 'chan', split_axis=0, concat_axis=2, tiled=True)  54 us
  transfers between devices with their start and end apart: 3, of which 1 were waited for; matrix products, arithmetic and copies ran while one was open for 77% of the time, Pallas kernels for 0%

commit v1 on v0

v1 whole, which is shorter than its diff:
```python
import functools

import jax
import jax.numpy as jnp
import numpy as np
from jax import lax
from jax.experimental import pallas as pl
from jax.experimental.pallas import tpu as pltpu
from jax.sharding import PartitionSpec as P

step_h = 0.25
step_tau = 0.02
row_start = 2.0
box_first = 8.0
lvalues = 4
lanes = 128
vmem_bytes = 56 * 1024 * 1024


def solve_tables(length):
    first_h = box_first / length
    radius = (np.arange(length) + 1.0) * first_h
    off = -step_tau / (4.0 * first_h * first_h)
    tiles = length // lanes
    groups = np.zeros((5, lvalues, tiles, lanes))
    for lvalue in range(lvalues):
        pot = -2.0 / radius + lvalue * (lvalue + 1.0) / (2.0 * radius * radius)
        diag = 1.0 + 0.5 * step_tau * (1.0 / (first_h * first_h) + pot)
        before, ratio = np.zeros(length), np.zeros(length)
        last = 1.0
        for j in range(length):
            before[j] = last
            last = -off / (diag[j] + (off * last if j else 0.0))
            ratio[j] = last
        ratio = ratio.reshape(tiles, lanes)
        down = np.cumprod(before.reshape(tiles, lanes), axis=1)
        up = np.cumprod(ratio[:, ::-1], axis=1)[:, ::-1]
        groups[0, lvalue] = 1.0 / down
        groups[1, lvalue] = down * ratio / up
        groups[2, lvalue] = down[:, -1:]
        groups[3, lvalue] = up
        groups[4, lvalue] = up[:, :1]
    tables = groups.transpose(2, 0, 1, 3).reshape(tiles, 5 * lvalues, lanes)
    return tables.astype(np.float32), -off


def sum_weights():
    upper = np.triu(np.ones((lanes, lanes)))
    whole = np.ones((lanes, lanes))
    return np.stack([np.hstack([upper, whole]), np.hstack([upper.T, whole])])


def pick(rows, group, which):
    first = group * lvalues
    chosen = rows[first + lvalues - 1:first + lvalues]
    for lvalue in range(lvalues - 2, -1, -1):
        chosen = jnp.where(which == lvalue, rows[first + lvalue:first + lvalue + 1], chosen)
    return chosen


def tile_sums(scaled_ref, sums_ref, weight):
    for n in range(scaled_ref.shape[0]):
        size = min(256, scaled_ref.shape[1])
        for start in range(0, scaled_ref.shape[1], size):
            value = scaled_ref[n, start:start + size]
            total = None
            for _ in range(3):
                part = value.astype(jnp.bfloat16)
                value = value - part.astype(jnp.float32)
                term = jnp.dot(part, weight, preferred_element_type=jnp.float32)
                total = term if total is None else total + term
            sums_ref[n, start:start + size] = total


def solve_kernel(with_rim, scale, rad_ref, channels_ref, pots_ref, table_ref, weights_ref, *refs):
    refs = list(refs)
    sums_ref, scaled_ref, psi_ref = refs.pop(), refs.pop(), refs.pop()
    source_ref = refs.pop(0)
    rim_ref = refs.pop(0) if with_rim else None
    out_ref = refs.pop(0)
    nrows, tiles, nchan, _ = psi_ref.shape
    rad = rad_ref[0]
    which = channels_ref[...]
    side = step_tau / (2.0 * step_h * step_h)

    def columns_of(tile):
        return pl.ds(pl.multiple_of(tile * lanes, lanes), lanes)

    def rows_of(tile):
        return pl.ds(pl.multiple_of(tile * nchan, nchan), nchan)

    def fields_of(tile):
        columns = columns_of(tile)
        if with_rim:
            rim = side * rim_ref[:, columns]
            return [
                source_ref[0, :, columns] + jnp.where(rad == 0, 0.0, rim),
                source_ref[1, :, columns] + jnp.where(rad == 0, rim, 0.0),
            ]
        edge_ref, outer_ref = refs
        count = source_ref.shape[1]
        rows = [source_ref[:, r, columns] for r in range(count)]
        edge_ref[:, columns] = jnp.where(rad == 0, rows[-1], rows[0])
        centre = [
            (1.0 - 2.0 * side - step_tau * pots_ref[r]) * rows[r] for r in range(count)
        ]
        outer_ref[0, :, columns] = centre[0] + side * rows[1]
        outer_ref[1, :, columns] = centre[-1] + side * rows[-2]
        return [centre[r] + side * (rows[r - 1] + rows[r + 1]) for r in range(1, count - 1)]

    @pl.loop(0, tiles, unroll=4)
    def _(tile):
        fields = fields_of(tile)
        inverse = pick(table_ref[tile], 0, which)
        for n in range(nrows):
            psi_ref[n, tile] = fields[n]
            scaled_ref[n, rows_of(tile)] = fields[n] * inverse

    def forward(tile, carry):
        rows = table_ref[tile]
        both, decay = pick(rows, 1, which), pick(rows, 2, which)
        after = []
        for n in range(nrows):
            sums = sums_ref[n, rows_of(tile)]
            scaled_ref[n, rows_of(tile)] = both * (sums[:, :lanes] + carry[n])
            after.append(decay * (sums[:, lanes:] + carry[n]))
        return tuple(after)

    def backward(step, carry):
        tile = tiles - 1 - step
        rows = table_ref[tile]
        product, decay = pick(rows, 3, which), pick(rows, 4, which)
        after = []
        for n in range(nrows):
            sums = sums_ref[n, rows_of(tile)]
            solved = product * (sums[:, :lanes] + carry[n])
            psi_ref[n, tile] = scale * solved - psi_ref[n, tile]
            after.append(decay * (sums[:, lanes:] + carry[n]))
        return tuple(after)

    zero = tuple(jnp.zeros((nchan, lanes), jnp.float32) for _ in range(nrows))
    tile_sums(scaled_ref, sums_ref, weights_ref[0])
    lax.fori_loop(0, tiles, forward, zero, unroll=4)
    tile_sums(scaled_ref, sums_ref, weights_ref[1])
    lax.fori_loop(0, tiles, backward, zero, unroll=4)
    for n in range(nrows):
        for tile in range(tiles):
            if out_ref.ndim == 4:
                per = out_ref.shape[-1] // lanes
                column = (tile % per) * lanes
                out_ref[tile // per, n, :, column:column + lanes] = psi_ref[n, tile]
            else:
                out_ref[n, :, tile * lanes:(tile + 1) * lanes] = psi_ref[n, tile]


def solve_rows(count, place, which, pots, source, rim, parts):
    nchan, length = which.shape[0], source.shape[-1]
    tables, off = solve_tables(length)
    tiles, block = length // lanes, length // parts
    aligned = block % lanes == 0
    piece = (parts, count, nchan, block) if aligned else (count, nchan, length)
    outs = [jax.ShapeDtypeStruct(piece, jnp.float32)]
    operands = [place, which, pots, jnp.asarray(tables), jnp.asarray(sum_weights(), jnp.bfloat16)]
    operands.append(source)
    if rim is None:
        outs.append(jax.ShapeDtypeStruct((nchan, length), jnp.float32))
        outs.append(jax.ShapeDtypeStruct((2, nchan, length), jnp.float32))
    else:
        operands.append(rim)
    vmem = pl.BlockSpec(memory_space=pltpu.VMEM)
    results = pl.pallas_call(
        functools.partial(solve_kernel, rim is not None, 2.0 / off),
        out_shape=outs,
        in_specs=[pl.BlockSpec(memory_space=pltpu.SMEM)] + [vmem] * (len(operands) - 1),
        out_specs=[vmem] * len(outs),
        scratch_shapes=[
            pltpu.VMEM((count, tiles, nchan, lanes), jnp.float32),
            pltpu.VMEM((count, tiles * nchan, lanes), jnp.float32),
            pltpu.VMEM((count, tiles * nchan, 2 * lanes), jnp.float32),
        ],
        compiler_params=pltpu.CompilerParams(vmem_limit_bytes=vmem_bytes),
        cost_estimate=pl.CostEstimate(
            flops=200 * source.size, bytes_accessed=16 * source.size, transcendentals=0
        ),
        name="solve_rim" if rim is not None else "solve_inner",
    )(*operands)
    pieces = results[0]
    if not aligned:
        pieces = jnp.transpose(pieces.reshape(count, nchan, parts, block), (2, 0, 1, 3))
    return [pieces] + list(results[1:])


def mats_kernel(coupling_ref, column_ref, row_ref, out_ref):
    raw = coupling_ref[0]
    total = raw.shape[0]
    same = column_ref[...] == row_ref[...]
    mat = jnp.where(same, 0.5 * (raw + raw.T), 0.0)
    high = mat.astype(jnp.bfloat16)
    low = (mat - high.astype(jnp.float32)).astype(jnp.bfloat16)
    out_ref[0, :, 0:total] = high
    out_ref[0, :, total:2 * total] = high
    out_ref[0, :, 2 * total:3 * total] = low


def split_mats(coupling, channels):
    orders, total, _ = coupling.shape
    group = channels[:, 2]
    return pl.pallas_call(
        mats_kernel,
        grid=(orders,),
        out_shape=jax.ShapeDtypeStruct((orders, total, 3 * total), jnp.bfloat16),
        in_specs=[
            pl.BlockSpec((1, total, total), lambda k: (k, 0, 0)),
            pl.BlockSpec((total, 1), lambda k: (0, 0)),
            pl.BlockSpec((1, total), lambda k: (0, 0)),
        ],
        out_specs=pl.BlockSpec((1, total, 3 * total), lambda k: (k, 0, 0)),
        compiler_params=pltpu.CompilerParams(vmem_limit_bytes=vmem_bytes),
        cost_estimate=pl.CostEstimate(
            flops=4 * coupling.size, bytes_accessed=10 * coupling.size, transcendentals=0
        ),
        name="split_mats",
    )(coupling, group[:, None], group[None, :])


def repel_kernel(points_ref, mats_ref, factors_ref, out_ref, field_ref, parts_ref):
    orders, total, _ = mats_ref.shape
    groups, count, nchan, block = points_ref.shape
    chunk = min(256, total)

    def put(slot, start, value):
        high = value.astype(jnp.bfloat16)
        low = (value - high.astype(jnp.float32)).astype(jnp.bfloat16)
        size = value.shape[0]
        parts_ref[slot, start:start + size] = high
        parts_ref[slot, total + start:total + start + size] = low
        parts_ref[slot, 2 * total + start:2 * total + start + size] = high

    weights = (-step_tau, step_tau * step_tau / 2.0, -step_tau * step_tau * step_tau / 6.0)
    for n in range(count):
        for group in range(groups):
            field_ref[group * nchan:(group + 1) * nchan] = points_ref[group, n]
        for start in range(0, total, chunk):
            put(0, start, field_ref[start:start + chunk])
        for stage, weight in enumerate(weights):
            slot = stage % 2
            for start in range(0, total, chunk):
                rows = slice(start, start + chunk)
                value = None
                for k in range(orders):
                    term = factors_ref[n, k:k + 1] * jnp.dot(
                        mats_ref[k, rows], parts_ref[slot], preferred_element_type=jnp.float32
                    )
                    value = term if value is None else value + term
                if stage < 2:
                    put(1 - slot, start, value)
                field_ref[rows] += weight * value
        for group in range(groups):
            out_ref[group, n] = field_ref[group * nchan:(group + 1) * nchan]


def repel(points, mats, factors):
    groups, count, nchan, block = points.shape
    orders, total, _ = mats.shape
    vmem = pl.BlockSpec(memory_space=pltpu.VMEM)
    return pl.pallas_call(
        repel_kernel,
        out_shape=jax.ShapeDtypeStruct(points.shape, jnp.float32),
        in_specs=[vmem] * 3,
        out_specs=vmem,
        scratch_shapes=[
            pltpu.VMEM((total, block), jnp.float32),
            pltpu.VMEM((2, 3 * total, block), jnp.bfloat16),
        ],
        compiler_params=pltpu.CompilerParams(vmem_limit_bytes=vmem_bytes),
        cost_estimate=pl.CostEstimate(
            flops=3 * orders * 3 * 2 * total * points.size,
            bytes_accessed=2 * mats.size + 8 * points.size,
            transcendentals=0,
        ),
        name="repel",
    )(points, mats, factors)


def gather_kernel(places, *refs):
    out_ref = refs[-1]
    nchan, rows, length = out_ref.shape
    for row, (source, n) in enumerate(places):
        ref = refs[source]
        for tile in range(length // lanes):
            columns = slice(tile * lanes, (tile + 1) * lanes)
            if ref.ndim == 4:
                per = ref.shape[-1] // lanes
                column = (tile % per) * lanes
                values = ref[tile // per, n, :, column:column + lanes]
            else:
                values = ref[n, :, columns]
            out_ref[:, row, columns] = values


def gather_rows(pieces, places, shape):
    nchan, rows, length = shape
    operands = []
    for piece in pieces:
        parts, count, _, block = piece.shape
        if block % lanes:
            piece = jnp.transpose(piece, (1, 2, 0, 3)).reshape(count, nchan, length)
        operands.append(piece)
    vmem = pl.BlockSpec(memory_space=pltpu.VMEM)
    return pl.pallas_call(
        functools.partial(gather_kernel, places),
        out_shape=jax.ShapeDtypeStruct(shape, jnp.float32),
        in_specs=[vmem] * len(operands),
        out_specs=vmem,
        compiler_params=pltpu.CompilerParams(vmem_limit_bytes=vmem_bytes),
        cost_estimate=pl.CostEstimate(
            flops=0, bytes_accessed=8 * nchan * rows * length, transcendentals=0
        ),
        name="gather_rows",
    )(*operands)


def potential(lvalue, radius):
    return -2.0 / radius + lvalue * (lvalue + 1.0) / (2.0 * radius * radius)


def radial_factors(rfirst, rsecond):
    rmin = jnp.minimum(rsecond[:, None], rfirst[None, :])
    rmax = jnp.maximum(rsecond[:, None], rfirst[None, :])
    return jnp.stack(
        [1.0 / rmax, rmin / (rmax * rmax), rmin * rmin / (rmax * rmax * rmax)], axis=1
    )


def swap_halves(part, axis, devices):
    return lax.ppermute(part, axis, [(i, (i + devices // 2) % devices) for i in range(devices)])


def on_device(parts, rads, wave, coupling, channels):
    nchan, rows, length = wave.shape
    chan_index = lax.axis_index("chan")
    rad_index = lax.axis_index("rad")
    place = jnp.reshape(rad_index, (1,)).astype(jnp.int32)
    mine = lax.dynamic_slice_in_dim(channels, chan_index * nchan, nchan)
    which = jnp.broadcast_to(mine[:, 0:1], (nchan, lanes))
    rsecond = (rad_index * rows + jnp.arange(rows) + 1).astype(jnp.float32) * step_h + row_start
    pots = potential(mine[:, 1].astype(jnp.float32)[None, :], rsecond[:, None])
    pots = jnp.broadcast_to(pots[:, :, None], (rows, nchan, lanes))
    block = length // parts
    points = (chan_index * block + jnp.arange(block) + 1).astype(jnp.float32) * (box_first / length)
    factors = radial_factors(points, rsecond)
    mats = split_mats(coupling, channels)

    inner = tuple(range(1, rows - 1))
    outer = (0, rows - 1)
    more = -nchan % 8
    which = jnp.pad(which, ((0, more), (0, 0)))
    pots = jnp.pad(pots, ((0, 0), (0, more), (0, 0)))
    padded = jnp.pad(wave, ((0, more), (0, 0), (0, 0))) if more else wave
    first, edge, partial = solve_rows(len(inner), place, which, pots, padded, None, parts)
    rim = swap_halves(edge, "rad", rads)
    second, = solve_rows(len(outer), place, which, pots, partial, rim, parts)
    if more:
        first, second = first[:, :, :nchan], second[:, :, :nchan]

    def exchange(pieces):
        return lax.all_to_all(pieces, "chan", 0, 0, tiled=True)

    results = []
    for rows_here, pieces in ((inner, first), (outer, second)):
        chosen = jnp.stack([factors[r] for r in rows_here])
        results.append(exchange(repel(exchange(pieces), mats, chosen)))
    order = {r: (0, n) for n, r in enumerate(inner)}
    order.update({r: (1, n) for n, r in enumerate(outer)})
    places = tuple(order[r] for r in range(rows))
    return gather_rows(results, places, wave.shape)


def solution(mesh):
    in_specs = (P("chan", "rad", None), P(), P())
    out_specs = P("chan", "rad", None)
    return jax.shard_map(
        functools.partial(on_device, mesh.shape["chan"], mesh.shape["rad"]),
        mesh=mesh,
        in_specs=in_specs,
        out_specs=out_specs,
        check_vma=False,
    )
```

time: 1490 us -> 140 us (0.09); the launches traced: 1460 us -> 139 us
  other arithmetic: 673 us -> 0.83 us
  local copies, waits for them, and re-layouts: 533 us -> 5.74 us
  matrix products: 145 us -> 0 us
  Pallas kernels: 0 us -> 48.9 us
  blocking collectives: 54 us -> 30.5 us
    while x228 -> x0, other arithmetic: 364 us -> none
    concatenate x5 -> x0, local copies, waits for them, and re-layouts: 205 us -> none  [solve_tables(): inverse = lax.linalg.tridiagonal_solve(below, centre, above, unit)]
    dot_general x11 -> x0, matrix products: 145 us -> none  [the longest x1 108 us: blocked_solve(): jnp.einsum('cbik,crbk->crbi', inverse, interior, precision=lax.Precision....]
    unnamed x83 -> x0, other arithmetic: 104 us -> none
    slice x1 -> x0, other arithmetic: 80.5 us -> none  [blocked_solve(): column_first = inverse[:, :, :, 1]]
    dynamic_update_slice x9 -> x0, local copies, waits for them, and re-layouts: 79.4 us -> none  [solve_tables(): inverse = lax.linalg.tridiagonal_solve(below, centre, above, unit)]
    unnamed x320 -> x9, local copies, waits for them, and re-layouts: 59.4 us -> 1.71 us
    slice x14 -> x0, local copies, waits for them, and re-layouts: 54.2 us -> none  [the longest x10 49.3 us: solve_tables(): inverse = lax.linalg.tridiagonal_solve(below, centre, above, unit)]
  transfers between devices with their start and end apart: 3 -> 4, of which waited for: 1 -> 4; matrix products, arithmetic and copies ran while one was open for 77% -> 3% of each run, Pallas kernels for 0% -> 24%
where the time goes in v1:
time: 140 us; the launch traced here: 139 us
  Pallas kernels  48.9 us (35%)
  waiting for transfers between devices  35.2 us (25%)
  blocking collectives  30.5 us (22%)
  starting transfers between devices  17.8 us (13%)
  local copies, waits for them, and re-layouts  5.74 us (4%)
    all_to_all x1, blocking collectives, exchange(): return lax.all_to_all(pieces, 'chan', 0, 0, tiled=True)  30.5 us
    all_to_all x3, waiting for transfers between devices, exchange(): return lax.all_to_all(pieces, 'chan', 0, 0, tiled=True)  23.1 us
    pallas_call x2, Pallas kernels, repel(): pl.pallas_call(repel_kernel, out_shape=jax.ShapeDtypeStruct(points.shape,...  23 us
    all_to_all x3, starting transfers between devices, exchange(): return lax.all_to_all(pieces, 'chan', 0, 0, tiled=True)  16.5 us
    pallas_call x2, Pallas kernels, solve_rows(): pl.pallas_call(functools.partial(solve_kernel, rim is not None, 2.0 / off...  15.9 us
    ppermute x1, waiting for transfers between devices, swap_halves(): lax.ppermute(part, axis, [(i, (i + devices // 2) % devices) for i in rang...  12.1 us
    pallas_call x1, Pallas kernels, split_mats(): pl.pallas_call(mats_kernel, grid=(orders,), out_shape=jax.ShapeDtypeStruc...  5.33 us
    pallas_call x1, Pallas kernels, gather_rows(): pl.pallas_call(functools.partial(gather_kernel, places), out_shape=jax.Sh...  4.75 us
  transfers between devices with their start and end apart: 4, of which 4 were waited for; matrix products, arithmetic and copies ran while one was open for 3% of the time, Pallas kernels for 24%

profile of v1, /device:TPU:9, one launch (start us, length us, event | category | flops | bytes accessed | tf_op | source)
XLA Modules:
  0.0 138.9 jit_solution(16786499472659284778)
XLA Ops:
  0.0 0.8 constant_dynamic-slice_fusion
  0.8 0.1 divide_add_fusion
  0.9 0.7 broadcast_in_dim.7.channels_ref
  1.5 0.7 broadcast_in_dim.8.pots_ref
  2.2 10.4 %solve_inner.1 = (f32[16,2,32,256]{3,2,1,0:T(8,128)}, f32[32,4096]{1,0:T(8,128)}, f32[2,32,4096]{2,1,0:T(8,128)}) custom-call(s32[1]{0:T(128)} %bitcast.rad_ref, s32[32,128]{1,0:T(8,128)} %broadcast_in_dim.7.channels_ref, f32[4,32,128]{2,1,0:T(8,128)} %broadcast_in_dim.8.pots_ref, f32[32,20,128]{2,1,0:T(8,128)} %constant.38.clone.table_ref, ...), custom_call_target="tpu_custom_call" | custom-call | flops 104857600 | bytes 8388608 | tf_op jit(solution)/shard_map/solve_inner/pallas_call | solution.py:171
  12.6 6.6 %all-to-all-start = ((f32[16,2,32,256]{3,2,1,0:T(8,128)}), f32[16,2,32,256]{3,2,1,0:T(8,128)S(1)}, u32[]{:S(2)}, u32[]{:S(2)}) async-start(f32[16,2,32,256]{3,2,1,0:T(8,128)} %get-tuple-element.8), calls=%async_computation | async-start | bytes 2097152 | tf_op jit(solution)/shard_map/all_to_all | solution.py:367
  19.2 1.2 collective-permute-start
  20.5 12.1 %collective-permute-done.refs_1_ = f32[32,4096]{1,0:T(8,128)S(1)} collective-permute-done((f32[32,4096]{1,0:T(8,128)}, f32[32,4096]{1,0:T(8,128)S(1)}, u32[]{:S(2)}, u32[]{:S(2)}) %collective-permute-start) | collective-permute-done | bytes 524320 | tf_op jit(solution)/shard_map/ppermute | solution.py:336
  32.6 0.0 copy-start.3
  32.6 0.8 copy-done.3
  33.4 5.5 %solve_rim.1 = f32[16,2,32,256]{3,2,1,0:T(8,128)} custom-call(s32[1]{0:T(128)} %bitcast.rad_ref, s32[32,128]{1,0:T(8,128)} %broadcast_in_dim.7.channels_ref, f32[4,32,128]{2,1,0:T(8,128)} %broadcast_in_dim.8.pots_ref, f32[32,20,128]{2,1,0:T(8,128)} %constant.38.clone.table_ref, bf16[2,128,256]{2,1,0:T(8,128)(2,1)} %constant.39.clone.weights_ref, ...), custom_call_target="tpu_custom_call" | custom-call | flops 52428800 | bytes 4194304 | tf_op jit(solution)/shard_map/solve_rim/pallas_call | solution.py:171
  38.9 5.2 %all-to-all-done.points_ref = f32[16,2,32,256]{3,2,1,0:T(8,128)S(1)} async-done(((f32[16,2,32,256]{3,2,1,0:T(8,128)}), f32[16,2,32,256]{3,2,1,0:T(8,128)S(1)}, u32[]{:S(2)}, u32[]{:S(2)}) %all-to-all-start) | async-done | bytes 1048608 | tf_op jit(solution)/shard_map/all_to_all | solution.py:367
  44.1 0.0 copy-start.1
  44.1 5.0 %all-to-all-start.2 = ((f32[16,2,32,256]{3,2,1,0:T(8,128)}), f32[16,2,32,256]{3,2,1,0:T(8,128)S(1)}, u32[]{:S(2)}, u32[]{:S(2)}) async-start(f32[16,2,32,256]{3,2,1,0:T(8,128)} %solve_rim.1), calls=%async_computation.2 | async-start | bytes 2097152 | tf_op jit(solution)/shard_map/all_to_all | solution.py:367
  49.1 0.1 maximum_divide_fusion
  49.2 0.6 stack.15.factors_ref
  49.8 1.3 slice_bitcast_fusion.1
  51.1 0.9 copy.12.column_ref
  52.0 5.3 %split_mats.1.mats_ref = bf16[3,512,1536]{2,1,0:T(8,128)(2,1)} custom-call(f32[3,512,512]{2,1,0:T(8,128)} %coupling_ref.1, s32[512,1]{1,0:T(8,128)} %copy.12.column_ref, s32[1,512]{1,0:T(1,128)} %get-tuple-element.11.row_ref), custom_call_target="tpu_custom_call" | custom-call | flops 3145728 | bytes 7864320 | tf_op jit(solution)/shard_map/split_mats/pallas_call | solution.py:208
  57.3 0.0 copy-done.1
  57.3 11.5 %repel.2 = f32[16,2,32,256]{3,2,1,0:T(8,128)} custom-call(f32[16,2,32,256]{3,2,1,0:T(8,128)} %copy-done.1, bf16[3,512,1536]{2,1,0:T(8,128)(2,1)} %split_mats.1.mats_ref, f32[2,3,256]{2,1,0:T(4,128)} %stack.15.factors_ref), custom_call_target="tpu_custom_call" | custom-call | flops 7247757312 | bytes 6815744 | tf_op jit(solution)/shard_map/repel/pallas_call | solution.py:266
  68.8 5.2 %all-to-all-done.2.points_ref = f32[16,2,32,256]{3,2,1,0:T(8,128)S(1)} async-done(((f32[16,2,32,256]{3,2,1,0:T(8,128)}), f32[16,2,32,256]{3,2,1,0:T(8,128)S(1)}, u32[]{:S(2)}, u32[]{:S(2)}) %all-to-all-start.2) | async-done | bytes 1048608 | tf_op jit(solution)/shard_map/all_to_all | solution.py:367
  73.9 0.0 copy-start.2
  73.9 5.0 %all-to-all-start.1 = ((f32[16,2,32,256]{3,2,1,0:T(8,128)}), f32[16,2,32,256]{3,2,1,0:T(8,128)S(1)}, u32[]{:S(2)}, u32[]{:S(2)}) async-start(f32[16,2,32,256]{3,2,1,0:T(8,128)} %repel.2), calls=%async_computation.1 | async-start | bytes 2097152 | tf_op jit(solution)/shard_map/all_to_all | solution.py:367
  78.9 0.6 fusion.factors_ref
  79.5 0.0 copy-done.2
  79.5 11.5 %repel.3 = f32[16,2,32,256]{3,2,1,0:T(8,128)} custom-call(f32[16,2,32,256]{3,2,1,0:T(8,128)} %copy-done.2, bf16[3,512,1536]{2,1,0:T(8,128)(2,1)} %split_mats.1.mats_ref, f32[2,3,256]{2,1,0:T(4,128)} %fusion.factors_ref), custom_call_target="tpu_custom_call" | custom-call | flops 7247757312 | bytes 6815744 | tf_op jit(solution)/shard_map/repel/pallas_call | solution.py:266
  91.0 12.7 %all-to-all-done.1.refs_0_ = f32[16,2,32,256]{3,2,1,0:T(8,128)S(1)} async-done(((f32[16,2,32,256]{3,2,1,0:T(8,128)}), f32[16,2,32,256]{3,2,1,0:T(8,128)S(1)}, u32[]{:S(2)}, u32[]{:S(2)}) %all-to-all-start.1) | async-done | bytes 1048608 | tf_op jit(solution)/shard_map/all_to_all | solution.py:367
  103.7 0.0 copy-start
  103.7 30.5 %all_to_all.20.refs_1_ = f32[16,2,32,256]{3,2,1,0:T(8,128)} all-to-all(f32[16,2,32,256]{3,2,1,0:T(8,128)} %repel.3), channel_id=1, replica_groups=mesh['rad'=2,'chan'=16] {'chan'}, dimensions={0} | all-to-all | bytes 2097152 | tf_op jit(solution)/shard_map/all_to_all | solution.py:367
  134.2 0.0 copy-done
  134.2 4.8 %gather_rows.1 = f32[32,4,4096]{2,1,0:T(4,128)} custom-call(f32[16,2,32,256]{3,2,1,0:T(8,128)} %copy-done, f32[16,2,32,256]{3,2,1,0:T(8,128)} %all_to_all.20.refs_1_), custom_call_target="tpu_custom_call" | custom-call | bytes 4194304 | tf_op jit(solution)/shard_map/gather_rows/pallas_call | solution.py:310
  (6 shorter events, 0.1 us)
Async XLA Ops:
  12.6 31.4 %all-to-all-start = ((f32[16,2,32,256]{3,2,1,0:T(8,128)}), f32[16,2,32,256]{3,2,1,0:T(8,128)S(1)}, u32[]{:S(2)}, u32[]{:S(2)}) async-start(f32[16,2,32,256]{3,2,1,0:T(8,128)} %get-tuple-element.8), calls=%async_computation | async-start | bytes 2097152 | tf_op jit(solution)/shard_map/all_to_all | solution.py:367
  19.2 13.4 %collective-permute-start = (f32[32,4096]{1,0:T(8,128)}, f32[32,4096]{1,0:T(8,128)S(1)}, u32[]{:S(2)}, u32[]{:S(2)}) collective-permute-start(f32[32,4096]{1,0:T(8,128)} %get-tuple-element.10), channel_id=1, source_target_pairs={{0,16},{16,0},{1,17},{17,1},{2,18},{18,2},{3,19},{19,3},{4,20},{20... | collective-permute-start | bytes 1572872 | tf_op jit(solution)/shard_map/ppermute | solution.py:336
  32.6 0.8 copy-start.3
  44.1 13.2 %copy-start.1 = (f32[16,2,32,256]{3,2,1,0:T(8,128)}, f32[16,2,32,256]{3,2,1,0:T(8,128)S(1)}, u32[]{:S(2)}) copy-start(f32[16,2,32,256]{3,2,1,0:T(8,128)S(1)} %all-to-all-done.points_ref) | copy-start | bytes 3145732
  44.1 29.8 %all-to-all-start.2 = ((f32[16,2,32,256]{3,2,1,0:T(8,128)}), f32[16,2,32,256]{3,2,1,0:T(8,128)S(1)}, u32[]{:S(2)}, u32[]{:S(2)}) async-start(f32[16,2,32,256]{3,2,1,0:T(8,128)} %solve_rim.1), calls=%async_computation.2 | async-start | bytes 2097152 | tf_op jit(solution)/shard_map/all_to_all | solution.py:367
  73.9 5.6 %copy-start.2 = (f32[16,2,32,256]{3,2,1,0:T(8,128)}, f32[16,2,32,256]{3,2,1,0:T(8,128)S(1)}, u32[]{:S(2)}) copy-start(f32[16,2,32,256]{3,2,1,0:T(8,128)S(1)} %all-to-all-done.2.points_ref) | copy-start | bytes 3145732
  73.9 29.8 %all-to-all-start.1 = ((f32[16,2,32,256]{3,2,1,0:T(8,128)}), f32[16,2,32,256]{3,2,1,0:T(8,128)S(1)}, u32[]{:S(2)}, u32[]{:S(2)}) async-start(f32[16,2,32,256]{3,2,1,0:T(8,128)} %repel.2), calls=%async_computation.1 | async-start | bytes 2097152 | tf_op jit(solution)/shard_map/all_to_all | solution.py:367
  103.7 30.5 %copy-start = (f32[16,2,32,256]{3,2,1,0:T(8,128)}, f32[16,2,32,256]{3,2,1,0:T(8,128)S(1)}, u32[]{:S(2)}) copy-start(f32[16,2,32,256]{3,2,1,0:T(8,128)S(1)} %all-to-all-done.1.refs_0_) | copy-start | bytes 3145732

commit v2 on v1

v2 whole, which is shorter than its diff:
```python
import functools

import jax
import jax.numpy as jnp
import numpy as np
from jax import lax
from jax.experimental import pallas as pl
from jax.experimental.pallas import tpu as pltpu
from jax.sharding import PartitionSpec as P

step_h = 0.25
step_tau = 0.02
row_start = 2.0
box_first = 8.0
lvalues = 4
lanes = 128
vmem_bytes = 24 * 1024 * 1024
first_vmem_bytes = 60 * 1024 * 1024


def solve_tables(length):
    first_h = box_first / length
    radius = (np.arange(length) + 1.0) * first_h
    off = -step_tau / (4.0 * first_h * first_h)
    tiles = length // lanes
    groups = np.zeros((5, lvalues, tiles, lanes))
    for lvalue in range(lvalues):
        pot = -2.0 / radius + lvalue * (lvalue + 1.0) / (2.0 * radius * radius)
        diag = 1.0 + 0.5 * step_tau * (1.0 / (first_h * first_h) + pot)
        before, ratio = np.zeros(length), np.zeros(length)
        last = 1.0
        for j in range(length):
            before[j] = last
            last = -off / (diag[j] + (off * last if j else 0.0))
            ratio[j] = last
        ratio = ratio.reshape(tiles, lanes)
        down = np.cumprod(before.reshape(tiles, lanes), axis=1)
        up = np.cumprod(ratio[:, ::-1], axis=1)[:, ::-1]
        groups[0, lvalue] = 1.0 / down
        groups[1, lvalue] = down * ratio / up
        groups[2, lvalue] = down[:, -1:]
        groups[3, lvalue] = up
        groups[4, lvalue] = up[:, :1]
    tables = groups.transpose(2, 0, 1, 3).reshape(tiles, 5 * lvalues, lanes)
    return tables.astype(np.float32), -off


def sum_weights():
    upper = np.triu(np.ones((lanes, lanes)))
    whole = np.ones((lanes, lanes))
    return np.stack([np.hstack([upper, whole]), np.hstack([upper.T, whole])])


def pick(rows, group, which):
    first = group * lvalues
    chosen = rows[first + lvalues - 1:first + lvalues]
    for lvalue in range(lvalues - 2, -1, -1):
        chosen = jnp.where(which == lvalue, rows[first + lvalue:first + lvalue + 1], chosen)
    return chosen


def group_sums(value, weight):
    total = None
    for _ in range(3):
        part = value.astype(jnp.bfloat16)
        value = value - part.astype(jnp.float32)
        term = jnp.dot(part, weight, preferred_element_type=jnp.float32)
        total = term if total is None else total + term
    return total


def channel_numbers(channels_ref, column, first, nchan):
    place = lax.broadcasted_iota(jnp.int32, (nchan, lanes), 0)
    value = jnp.zeros((nchan, lanes), jnp.int32)
    count = min(nchan, channels_ref.shape[1])
    for n in range(count):
        index = jnp.minimum(first + n, channels_ref.shape[1] - 1)
        value = jnp.where(place == n, channels_ref[column, index], value)
    return value


def row_scale(channels_ref, first, nchan, row, rad, rows):
    number = channel_numbers(channels_ref, 1, first, nchan).astype(jnp.float32)
    radius = (rad * rows + row + 1).astype(jnp.float32) * step_h + row_start
    pot = potential(number, jnp.full((nchan, lanes), radius, jnp.float32))
    return (1.0 - step_tau / (step_h * step_h)) - step_tau * pot


def outer_kernel(chan_size, channels_ref, wave_ref, edge_ref, outer_ref):
    nchan, rows, length = wave_ref.shape
    side = step_tau / (2.0 * step_h * step_h)
    rad = lax.axis_index("rad")
    first = lax.axis_index("chan") * chan_size
    centre_first = row_scale(channels_ref, first, nchan, 0, rad, rows)
    centre_last = row_scale(channels_ref, first, nchan, rows - 1, rad, rows)
    for tile in range(length // lanes):
        columns = slice(tile * lanes, (tile + 1) * lanes)
        top, bottom = wave_ref[:, 0, columns], wave_ref[:, rows - 1, columns]
        edge_ref[:, columns] = jnp.where(rad == 0, bottom, top)
        outer_ref[0, :, columns] = centre_first * top + side * wave_ref[:, 1, columns]
        outer_ref[1, :, columns] = centre_last * bottom + side * wave_ref[:, rows - 2, columns]


def outer_rows(channels, wave, chan_size):
    nchan, rows, length = wave.shape
    vmem = pl.BlockSpec(memory_space=pltpu.VMEM)
    return pl.pallas_call(
        functools.partial(outer_kernel, chan_size),
        out_shape=[
            jax.ShapeDtypeStruct((nchan, length), jnp.float32),
            jax.ShapeDtypeStruct((2, nchan, length), jnp.float32),
        ],
        in_specs=[pl.BlockSpec(memory_space=pltpu.SMEM), vmem],
        out_specs=[vmem, vmem],
        compiler_params=pltpu.CompilerParams(vmem_limit_bytes=vmem_bytes),
        cost_estimate=pl.CostEstimate(
            flops=8 * wave.size, bytes_accessed=8 * wave.size, transcendentals=0
        ),
        name="outer_rows",
    )(channels, wave)


def solve_kernel(with_rim, chan_size, scale, channels_ref, table_ref, weights_ref, *refs):
    refs = list(refs)
    out_sems, stage_ref, psi_ref, ready_ref = refs.pop(), refs.pop(), refs.pop(), refs.pop()
    source_ref = refs.pop(0)
    rim_ref = refs.pop(0) if with_rim else None
    out_ref = refs.pop(0)
    nrows, tiles, nchan, _ = psi_ref.shape
    if not with_rim:
        rows_ref, in_sems = refs
    rad = lax.axis_index("rad")
    first = lax.axis_index("chan") * chan_size
    which = channel_numbers(channels_ref, 0, first, nchan)
    side = step_tau / (2.0 * step_h * step_h)
    groups = in_sems.shape[0] if not with_rim else out_sems.shape[0]
    group = tiles // groups

    def row_copies(step):
        columns = pl.ds(step * group * lanes, group * lanes)
        return [
            pltpu.make_async_copy(
                source_ref.at[:, r, columns], rows_ref.at[r, :, columns], in_sems.at[step, r]
            )
            for r in range(source_ref.shape[1])
        ]

    def out_copy(step):
        if out_ref.ndim == 4:
            here = pl.ds(step * (out_ref.shape[0] // groups), out_ref.shape[0] // groups)
            return pltpu.make_async_copy(ready_ref.at[here], out_ref.at[here], out_sems.at[step])
        here = pl.ds(step * group * lanes, group * lanes)
        return pltpu.make_async_copy(
            ready_ref.at[:, :, here], out_ref.at[:, :, here], out_sems.at[step]
        )

    if not with_rim:
        for step in range(groups):
            for copy in row_copies(step):
                copy.start()
        rows = source_ref.shape[1]
        scales = [row_scale(channels_ref, first, nchan, r, rad, rows) for r in range(1, rows - 1)]

    def fields_of(tile):
        columns = slice(tile * lanes, (tile + 1) * lanes)
        if with_rim:
            rim = side * rim_ref[:, columns]
            return [
                source_ref[0, :, columns] + jnp.where(rad == 0, 0.0, rim),
                source_ref[1, :, columns] + jnp.where(rad == 0, rim, 0.0),
            ]
        around = [rows_ref[r, :, columns] for r in range(rows)]
        return [
            scales[r - 1] * around[r] + side * (around[r - 1] + around[r + 1])
            for r in range(1, rows - 1)
        ]

    carry = [jnp.zeros((nchan, lanes), jnp.float32) for _ in range(nrows)]
    for start in range(0, tiles, group):
        if not with_rim:
            for copy in row_copies(start // group):
                copy.wait()
        scaled = [[] for _ in range(nrows)]
        for tile in range(start, start + group):
            fields = fields_of(tile)
            inverse = pick(table_ref[tile], 0, which)
            for n in range(nrows):
                psi_ref[n, tile] = fields[n]
                scaled[n].append(fields[n] * inverse)
        sums = [group_sums(jnp.concatenate(scaled[n], axis=0), weights_ref[0]) for n in range(nrows)]
        for tile in range(start, start + group):
            both, decay = pick(table_ref[tile], 1, which), pick(table_ref[tile], 2, which)
            here = slice((tile - start) * nchan, (tile - start + 1) * nchan)
            for n in range(nrows):
                stage_ref[n, tile * nchan:(tile + 1) * nchan] = both * (
                    sums[n][here, :lanes] + carry[n]
                )
                carry[n] = decay * (sums[n][here, lanes:] + carry[n])

    carry = [jnp.zeros((nchan, lanes), jnp.float32) for _ in range(nrows)]
    for start in range(tiles - group, -1, -group):
        rows_here = slice(start * nchan, (start + group) * nchan)
        sums = [group_sums(stage_ref[n, rows_here], weights_ref[1]) for n in range(nrows)]
        for tile in range(start + group - 1, start - 1, -1):
            product, decay = pick(table_ref[tile], 3, which), pick(table_ref[tile], 4, which)
            here = slice((tile - start) * nchan, (tile - start + 1) * nchan)
            for n in range(nrows):
                solved = product * (sums[n][here, :lanes] + carry[n])
                value = scale * solved - psi_ref[n, tile]
                if ready_ref.ndim == 4:
                    per = ready_ref.shape[-1] // lanes
                    column = (tile % per) * lanes
                    ready_ref[tile // per, n, :, column:column + lanes] = value
                else:
                    ready_ref[n, :, tile * lanes:(tile + 1) * lanes] = value
                carry[n] = decay * (sums[n][here, lanes:] + carry[n])
        out_copy(start // group).start()
    for step in range(groups):
        out_copy(step).wait()


def solve_rows(count, channels, source, rim, parts, chan_size):
    nchan, length = source.shape[0] if rim is None else source.shape[1], source.shape[-1]
    tables, off = solve_tables(length)
    tiles, block = length // lanes, length // parts
    aligned = block % lanes == 0
    piece = (parts, count, nchan, block) if aligned else (count, nchan, length)
    operands = [channels, jnp.asarray(tables), jnp.asarray(sum_weights(), jnp.bfloat16), source]
    if rim is not None:
        operands.append(rim)
    vmem = pl.BlockSpec(memory_space=pltpu.VMEM)
    anywhere = pl.BlockSpec(memory_space=pl.ANY)
    groups = 4
    scratch = [
        pltpu.VMEM(piece, jnp.float32),
        pltpu.VMEM((count, tiles, nchan, lanes), jnp.float32),
        pltpu.VMEM((count, tiles * nchan, lanes), jnp.float32),
        pltpu.SemaphoreType.DMA((groups,)),
    ]
    if rim is None:
        rows = source.shape[1]
        scratch = [
            pltpu.VMEM((rows, nchan, length), jnp.float32),
            pltpu.SemaphoreType.DMA((groups, rows)),
        ] + scratch
    pieces = pl.pallas_call(
        functools.partial(solve_kernel, rim is not None, chan_size, 2.0 / off),
        out_shape=jax.ShapeDtypeStruct(piece, jnp.float32),
        in_specs=[pl.BlockSpec(memory_space=pltpu.SMEM), vmem, vmem]
        + ([anywhere] if rim is None else [vmem, vmem]),
        out_specs=anywhere,
        scratch_shapes=scratch,
        compiler_params=pltpu.CompilerParams(
            vmem_limit_bytes=first_vmem_bytes if rim is None else vmem_bytes
        ),
        cost_estimate=pl.CostEstimate(
            flops=200 * source.size, bytes_accessed=16 * source.size, transcendentals=0
        ),
        name="solve_rim" if rim is not None else "solve_inner",
    )(*operands)
    if not aligned:
        pieces = jnp.transpose(pieces.reshape(count, nchan, parts, block), (2, 0, 1, 3))
    return pieces


def mats_kernel(coupling_ref, column_ref, row_ref, out_ref):
    raw = coupling_ref[0]
    total = raw.shape[0]
    same = column_ref[...] == row_ref[...]
    mat = jnp.where(same, 0.5 * (raw + raw.T), 0.0)
    high = mat.astype(jnp.bfloat16)
    low = (mat - high.astype(jnp.float32)).astype(jnp.bfloat16)
    out_ref[0, :, 0:total] = high
    out_ref[0, :, total:2 * total] = high
    out_ref[0, :, 2 * total:3 * total] = low


def split_mats(coupling, channels):
    orders, total, _ = coupling.shape
    group = channels[:, 2]
    return pl.pallas_call(
        mats_kernel,
        grid=(orders,),
        out_shape=jax.ShapeDtypeStruct((orders, total, 3 * total), jnp.bfloat16),
        in_specs=[
            pl.BlockSpec((1, total, total), lambda k: (k, 0, 0)),
            pl.BlockSpec((total, 1), lambda k: (0, 0)),
            pl.BlockSpec((1, total), lambda k: (0, 0)),
        ],
        out_specs=pl.BlockSpec((1, total, 3 * total), lambda k: (k, 0, 0)),
        compiler_params=pltpu.CompilerParams(vmem_limit_bytes=vmem_bytes),
        cost_estimate=pl.CostEstimate(
            flops=4 * coupling.size, bytes_accessed=10 * coupling.size, transcendentals=0
        ),
        name="split_mats",
    )(coupling, group[:, None], group[None, :])


def repel_kernel(points_ref, mats_ref, factors_ref, out_ref, field_ref, parts_ref):
    orders, total, _ = mats_ref.shape
    groups, count, nchan, block = points_ref.shape
    chunk = min(256, total)

    def put(slot, start, value):
        high = value.astype(jnp.bfloat16)
        low = (value - high.astype(jnp.float32)).astype(jnp.bfloat16)
        size = value.shape[0]
        parts_ref[slot, start:start + size] = high
        parts_ref[slot, total + start:total + start + size] = low
        parts_ref[slot, 2 * total + start:2 * total + start + size] = high

    weights = (-step_tau, step_tau * step_tau / 2.0, -step_tau * step_tau * step_tau / 6.0)
    for n in range(count):
        for group in range(groups):
            field_ref[group * nchan:(group + 1) * nchan] = points_ref[group, n]
        for start in range(0, total, chunk):
            put(0, start, field_ref[start:start + chunk])
        for stage, weight in enumerate(weights):
            slot = stage % 2
            for start in range(0, total, chunk):
                rows = slice(start, start + chunk)
                value = None
                for k in range(orders):
                    term = factors_ref[n, k:k + 1] * jnp.dot(
                        mats_ref[k, rows], parts_ref[slot], preferred_element_type=jnp.float32
                    )
                    value = term if value is None else value + term
                if stage < 2:
                    put(1 - slot, start, value)
                field_ref[rows] += weight * value
        for group in range(groups):
            out_ref[group, n] = field_ref[group * nchan:(group + 1) * nchan]


def repel(points, mats, factors):
    groups, count, nchan, block = points.shape
    orders, total, _ = mats.shape
    vmem = pl.BlockSpec(memory_space=pltpu.VMEM)
    return pl.pallas_call(
        repel_kernel,
        out_shape=jax.ShapeDtypeStruct(points.shape, jnp.float32),
        in_specs=[vmem] * 3,
        out_specs=vmem,
        scratch_shapes=[
            pltpu.VMEM((total, block), jnp.float32),
            pltpu.VMEM((2, 3 * total, block), jnp.bfloat16),
        ],
        compiler_params=pltpu.CompilerParams(vmem_limit_bytes=vmem_bytes),
        cost_estimate=pl.CostEstimate(
            flops=3 * orders * 3 * 2 * total * points.size,
            bytes_accessed=2 * mats.size + 8 * points.size,
            transcendentals=0,
        ),
        name="repel",
    )(points, mats, factors)


def gather_kernel(targets, piece_ref, *refs):
    sems = refs[-1]
    out_ref = refs[-2]
    length = out_ref.shape[-1]
    copies = []
    for n, row in enumerate(targets):
        if piece_ref.ndim == 4:
            parts, _, _, block = piece_ref.shape
            for part in range(parts):
                columns = pl.ds(part * block, block)
                copies.append((piece_ref.at[part, n], out_ref.at[:, row, columns]))
        else:
            copies.append((piece_ref.at[n], out_ref.at[:, row, :]))
    copies = [pltpu.make_async_copy(*ends, sems.at[k]) for k, ends in enumerate(copies)]
    for copy in copies:
        copy.start()
    for copy in copies:
        copy.wait()


def gather_rows(piece, targets, earlier, shape):
    nchan, rows, length = shape
    parts, count, _, block = piece.shape
    if block % lanes or nchan % 8:
        piece = jnp.transpose(piece, (1, 2, 0, 3)).reshape(count, nchan, length)
    anywhere = pl.BlockSpec(memory_space=pl.ANY)
    operands = [piece] if earlier is None else [piece, earlier]
    return pl.pallas_call(
        functools.partial(gather_kernel, targets),
        out_shape=jax.ShapeDtypeStruct(shape, jnp.float32),
        in_specs=[anywhere] * len(operands),
        out_specs=anywhere,
        scratch_shapes=[pltpu.SemaphoreType.DMA((count * parts,))],
        input_output_aliases={} if earlier is None else {1: 0},
        compiler_params=pltpu.CompilerParams(vmem_limit_bytes=vmem_bytes),
        cost_estimate=pl.CostEstimate(
            flops=0, bytes_accessed=4 * count * nchan * length, transcendentals=0
        ),
        name="gather_first" if earlier is None else "gather_last",
    )(*operands)


def potential(lvalue, radius):
    return -2.0 / radius + lvalue * (lvalue + 1.0) / (2.0 * radius * radius)


def radial_factors(rfirst, rsecond):
    rmin = jnp.minimum(rsecond[:, None], rfirst[None, :])
    rmax = jnp.maximum(rsecond[:, None], rfirst[None, :])
    return jnp.stack(
        [1.0 / rmax, rmin / (rmax * rmax), rmin * rmin / (rmax * rmax * rmax)], axis=1
    )


def swap_halves(part, axis, devices):
    return lax.ppermute(part, axis, [(i, (i + devices // 2) % devices) for i in range(devices)])


def on_device(parts, rads, wave, coupling, channels):
    nchan, rows, length = wave.shape
    rad_index, chan_index = lax.axis_index("rad"), lax.axis_index("chan")
    numbers = channels.T
    inner = tuple(range(1, rows - 1))
    outer = (0, rows - 1)
    more = -nchan % 8
    padded = jnp.pad(wave, ((0, more), (0, 0), (0, 0))) if more else wave

    def exchange(pieces):
        return lax.all_to_all(pieces, "chan", 0, 0, tiled=True)

    first = solve_rows(len(inner), numbers, padded, None, parts, nchan)
    edge, partial = outer_rows(numbers, padded, nchan)
    rim = swap_halves(edge, "rad", rads)
    second = solve_rows(len(outer), numbers, partial, rim, parts, nchan)
    if more:
        first, second = first[:, :, :nchan], second[:, :, :nchan]

    block = length // parts
    rsecond = (rad_index * rows + jnp.arange(rows) + 1).astype(jnp.float32) * step_h + row_start
    points = (chan_index * block + jnp.arange(block) + 1).astype(jnp.float32) * (box_first / length)
    factors = radial_factors(points, rsecond)
    mats = split_mats(coupling, channels)
    result = None
    for here, pieces in ((inner, first), (outer, second)):
        chosen = jnp.stack([factors[r] for r in here])
        pieces = exchange(repel(exchange(pieces), mats, chosen))
        result = gather_rows(pieces, here, result, wave.shape)
    return result


def solution(mesh):
    in_specs = (P("chan", "rad", None), P(), P())
    out_specs = P("chan", "rad", None)
    return jax.shard_map(
        functools.partial(on_device, mesh.shape["chan"], mesh.shape["rad"]),
        mesh=mesh,
        in_specs=in_specs,
        out_specs=out_specs,
        check_vma=False,
    )
```

time: 140 us -> 129 us (0.921)
  blocking collectives: 30.5 us -> 0 us
  waiting for transfers between devices: 35.2 us -> 64.1 us
  Pallas kernels: 48.9 us -> 36.5 us
  starting transfers between devices: 17.8 us -> 22.9 us
    all_to_all x1 -> x0, blocking collectives: 30.5 us -> none  [exchange(): return lax.all_to_all(pieces, 'chan', 0, 0, tiled=True)]
    all_to_all x3 -> x4, waiting for transfers between devices: 23.1 us -> 52 us  [exchange(): return lax.all_to_all(pieces, 'chan', 0, 0, tiled=True)]
    pallas_call x3 -> x5, Pallas kernels: 20.6 us -> 14.9 us  [the longest x2 9.3 us: solve_rows(): pl.pallas_call(functools.partial(solve_kernel, rim is not None, chan_size...]
    all_to_all x3 -> x4, starting transfers between devices: 16.5 us -> 21.7 us  [exchange(): return lax.all_to_all(pieces, 'chan', 0, 0, tiled=True)]
    pallas_call x1, Pallas kernels: 5.33 us -> 1.44 us  [split_mats(): pl.pallas_call(mats_kernel, grid=(orders,), out_shape=jax.ShapeDtypeStruc...]
    unnamed x9 -> x15, local copies, waits for them, and re-layouts: 1.71 us -> 4.62 us
    pallas_call x2, Pallas kernels: 23 us -> 20.1 us  [repel(): pl.pallas_call(repel_kernel, out_shape=jax.ShapeDtypeStruct(points.shape,...]
  transfers between devices with their start and end apart: 4 -> 5, of which waited for: 4 -> 5; matrix products, arithmetic and copies ran while one was open for 3% -> 0% of each run, Pallas kernels for 24% -> 23%
where the time goes in v2:
time: 129 us; the launch traced here: 128 us
  waiting for transfers between devices  64.1 us (50%)
  Pallas kernels  36.5 us (28%)
  starting transfers between devices  22.9 us (18%)
  local copies, waits for them, and re-layouts  4.63 us (4%)
    all_to_all x4, waiting for transfers between devices, exchange(): return lax.all_to_all(pieces, 'chan', 0, 0, tiled=True)  52 us
    all_to_all x4, starting transfers between devices, exchange(): return lax.all_to_all(pieces, 'chan', 0, 0, tiled=True)  21.7 us
    pallas_call x2, Pallas kernels, repel(): pl.pallas_call(repel_kernel, out_shape=jax.ShapeDtypeStruct(points.shape,...  20.1 us
    ppermute x1, waiting for transfers between devices, swap_halves(): lax.ppermute(part, axis, [(i, (i + devices // 2) % devices) for i in rang...  12 us
    pallas_call x2, Pallas kernels, solve_rows(): pl.pallas_call(functools.partial(solve_kernel, rim is not None, chan_size...  9.3 us
    unnamed x15, local copies, waits for them, and re-layouts  4.62 us
    pallas_call x1, Pallas kernels, outer_rows(): pl.pallas_call(functools.partial(outer_kernel, chan_size), out_shape=[jax...  3.15 us
  transfers between devices with their start and end apart: 5, of which 5 were waited for; matrix products, arithmetic and copies ran while one was open for 0% of the time, Pallas kernels for 23%

profile of v2, /device:TPU:9, one launch (start us, length us, event | category | flops | bytes accessed | tf_op | source)
XLA Modules:
  0.0 128.5 jit_solution(17162228673774511128)
XLA Ops:
  0.0 0.0 copy-start
  0.0 0.0 copy-start.6
  0.0 5.8 %solve_inner.1 = f32[16,2,32,256]{3,2,1,0:T(8,128)} custom-call(s32[3,512]{1,0:T(4,128)} %bitcast.4, f32[32,20,128]{2,1,0:T(8,128)} %constant.28.clone.table_ref, bf16[2,128,256]{2,1,0:T(8,128)(2,1)} %constant.29.clone.weights_ref, f32[32,4,4096]{2,1,0:T(4,128)} %refs_0_.1), custom_call_target="tpu_custom_call" | custom-call | flops 104857600 | bytes 8388608 | tf_op jit(solution)/shard_map/solve_inner/pallas_call | solution.py:246
  5.8 0.0 copy-start.4
  5.8 6.8 %all-to-all-start.2 = ((f32[16,2,32,256]{3,2,1,0:T(8,128)}), f32[16,2,32,256]{3,2,1,0:T(8,128)}, u32[]{:S(2)}, u32[]{:S(2)}) async-start(f32[16,2,32,256]{3,2,1,0:T(8,128)} %solve_inner.1), calls=%async_computation.2 | async-start | bytes 2097152 | tf_op jit(solution)/shard_map/all_to_all | solution.py:426
  12.6 0.0 copy-done
  12.6 0.0 copy-done.6
  12.6 0.0 copy-start.5
  12.6 3.1 %outer_rows.1 = (f32[32,4096]{1,0:T(8,128)S(1)}, f32[2,32,4096]{2,1,0:T(8,128)S(1)}) custom-call(s32[3,512]{1,0:T(4,128)S(1)} %bitcast.5, f32[32,4,4096]{2,1,0:T(4,128)S(1)} %copy-done), custom_call_target="tpu_custom_call" | custom-call | flops 4194304 | bytes 4194304 | tf_op jit(solution)/shard_map/outer_rows/pallas_call | solution.py:107
  15.8 1.3 collective-permute-start
  17.0 12.0 %collective-permute-done.refs_1_ = f32[32,4096]{1,0:T(8,128)S(1)} collective-permute-done((f32[32,4096]{1,0:T(8,128)S(1)}, f32[32,4096]{1,0:T(8,128)S(1)}, u32[]{:S(2)}, u32[]{:S(2)}) %collective-permute-start) | collective-permute-done | bytes 524320 | tf_op jit(solution)/shard_map/ppermute | solution.py:413
  29.1 0.0 copy-done.4
  29.1 0.0 copy-done.5
  29.1 0.0 copy-start.3
  29.1 3.5 %solve_rim.1 = f32[16,2,32,256]{3,2,1,0:T(8,128)} custom-call(s32[3,512]{1,0:T(4,128)S(1)} %bitcast.6, f32[32,20,128]{2,1,0:T(8,128)S(1)} %copy-done.4, bf16[2,128,256]{2,1,0:T(8,128)(2,1)S(1)} %copy-done.5, f32[2,32,4096]{2,1,0:T(8,128)S(1)} %get-tuple-element.7.refs_0_, f32[32,4096]{1,0:T(8,128)S(1)} %collective-permute-done.refs_1_), custom_call_target="tpu_custom_call" | custom-call | flops 52428800 | bytes 4194304 | tf_op jit(solution)/shard_map/solve_rim/pallas_call | solution.py:246
  32.6 5.0 %all-to-all-done.2.points_ref = f32[16,2,32,256]{3,2,1,0:T(8,128)} async-done(((f32[16,2,32,256]{3,2,1,0:T(8,128)}), f32[16,2,32,256]{3,2,1,0:T(8,128)}, u32[]{:S(2)}, u32[]{:S(2)}) %all-to-all-start.2) | async-done | bytes 1048608 | tf_op jit(solution)/shard_map/all_to_all | solution.py:426
  37.5 5.0 %all-to-all-start = ((f32[16,2,32,256]{3,2,1,0:T(8,128)}), f32[16,2,32,256]{3,2,1,0:T(8,128)}, u32[]{:S(2)}, u32[]{:S(2)}) async-start(f32[16,2,32,256]{3,2,1,0:T(8,128)} %solve_rim.1), calls=%async_computation | async-start | bytes 2097152 | tf_op jit(solution)/shard_map/all_to_all | solution.py:426
  42.5 0.1 copy.13.column_ref
  42.7 0.0 copy-done.3
  42.7 1.4 %split_mats.1.mats_ref = bf16[3,512,1536]{2,1,0:T(8,128)(2,1)S(1)} custom-call(f32[3,512,512]{2,1,0:T(8,128)S(1)} %copy-done.3, s32[512,1]{1,0:T(8,128)S(1)} %copy.13.column_ref, s32[1,512]{1,0:T(1,128)S(1)} %get-tuple-element.11.row_ref), custom_call_target="tpu_custom_call" | custom-call | flops 3145728 | bytes 7864320 | tf_op jit(solution)/shard_map/split_mats/pallas_call | solution.py:281
  44.2 0.1 maximum_divide_fusion
  44.3 10.1 %repel.3 = f32[16,2,32,256]{3,2,1,0:T(8,128)} custom-call(f32[16,2,32,256]{3,2,1,0:T(8,128)} %all-to-all-done.2.points_ref, bf16[3,512,1536]{2,1,0:T(8,128)(2,1)S(1)} %split_mats.1.mats_ref, f32[2,3,256]{2,1,0:T(4,128)S(1)} %get-tuple-element.9.factors_ref), custom_call_target="tpu_custom_call" | custom-call | flops 7247757312 | bytes 6815744 | tf_op jit(solution)/shard_map/repel/pallas_call | solution.py:339
  54.4 2.1 %copy-done.1 = bf16[3,512,1536]{2,1,0:T(8,128)(2,1)} copy-done((bf16[3,512,1536]{2,1,0:T(8,128)(2,1)}, bf16[3,512,1536]{2,1,0:T(8,128)(2,1)S(1)}, u32[]{:S(2)}) %copy-start.1) | copy-done | bytes 4718616
  56.5 11.0 %all-to-all-done.points_ref = f32[16,2,32,256]{3,2,1,0:T(8,128)} async-done(((f32[16,2,32,256]{3,2,1,0:T(8,128)}), f32[16,2,32,256]{3,2,1,0:T(8,128)}, u32[]{:S(2)}, u32[]{:S(2)}) %all-to-all-start) | async-done | bytes 1048608 | tf_op jit(solution)/shard_map/all_to_all | solution.py:426
  67.5 5.0 %all-to-all-start.3 = ((f32[16,2,32,256]{3,2,1,0:T(8,128)}), f32[16,2,32,256]{3,2,1,0:T(8,128)S(1)}, u32[]{:S(2)}, u32[]{:S(2)}) async-start(f32[16,2,32,256]{3,2,1,0:T(8,128)} %repel.3), calls=%async_computation.3 | async-start | bytes 2097152 | tf_op jit(solution)/shard_map/all_to_all | solution.py:426
  72.4 2.3 %copy-done.2 = bf16[3,512,1536]{2,1,0:T(8,128)(2,1)S(1)} copy-done((bf16[3,512,1536]{2,1,0:T(8,128)(2,1)S(1)}, bf16[3,512,1536]{2,1,0:T(8,128)(2,1)}, u32[]{:S(2)}) %copy-start.2) | copy-done | bytes 4718616
  74.8 10.1 %repel.2 = f32[16,2,32,256]{3,2,1,0:T(8,128)} custom-call(f32[16,2,32,256]{3,2,1,0:T(8,128)} %all-to-all-done.points_ref, bf16[3,512,1536]{2,1,0:T(8,128)(2,1)S(1)} %copy-done.2, f32[2,3,256]{2,1,0:T(4,128)S(1)} %get-tuple-element.10.factors_ref), custom_call_target="tpu_custom_call" | custom-call | flops 7247757312 | bytes 6815744 | tf_op jit(solution)/shard_map/repel/pallas_call | solution.py:339
  84.8 12.5 %all-to-all-done.3.piece_ref = f32[16,2,32,256]{3,2,1,0:T(8,128)S(1)} async-done(((f32[16,2,32,256]{3,2,1,0:T(8,128)}), f32[16,2,32,256]{3,2,1,0:T(8,128)S(1)}, u32[]{:S(2)}, u32[]{:S(2)}) %all-to-all-start.3) | async-done | bytes 1048608 | tf_op jit(solution)/shard_map/all_to_all | solution.py:426
  97.3 5.0 %all-to-all-start.1 = ((f32[16,2,32,256]{3,2,1,0:T(8,128)}), f32[16,2,32,256]{3,2,1,0:T(8,128)S(1)}, u32[]{:S(2)}, u32[]{:S(2)}) async-start(f32[16,2,32,256]{3,2,1,0:T(8,128)} %repel.2), calls=%async_computation.1 | async-start | bytes 2097152 | tf_op jit(solution)/shard_map/all_to_all | solution.py:426
  102.3 1.2 gather_first.1.refs_0_
  103.5 23.6 %all-to-all-done.1.piece_ref = f32[16,2,32,256]{3,2,1,0:T(8,128)S(1)} async-done(((f32[16,2,32,256]{3,2,1,0:T(8,128)}), f32[16,2,32,256]{3,2,1,0:T(8,128)S(1)}, u32[]{:S(2)}, u32[]{:S(2)}) %all-to-all-start.1) | async-done | bytes 1048608 | tf_op jit(solution)/shard_map/all_to_all | solution.py:426
  127.1 1.2 gather_last.1
  (6 shorter events, 0.0 us)
Async XLA Ops:
  0.0 12.6 %copy-start = (f32[32,4,4096]{2,1,0:T(4,128)S(1)}, f32[32,4,4096]{2,1,0:T(4,128)}, u32[]{:S(2)}) copy-start(f32[32,4,4096]{2,1,0:T(4,128)} %refs_0_.1) | copy-start | bytes 6291460
  0.0 12.6 %copy-start.6 = (s32[512,3]{0,1:T(4,128)S(1)}, s32[512,3]{0,1:T(4,128)}, u32[]{:S(2)}) copy-start(s32[512,3]{0,1:T(4,128)} %param.9) | copy-start | bytes 18436
  5.8 23.3 %copy-start.4 = (f32[32,20,128]{2,1,0:T(8,128)S(1)}, f32[32,20,128]{2,1,0:T(8,128)}, u32[]{:S(2)}) copy-start(f32[32,20,128]{2,1,0:T(8,128)} %constant.28.clone.table_ref) | copy-start | bytes 983044
  5.8 31.7 %all-to-all-start.2 = ((f32[16,2,32,256]{3,2,1,0:T(8,128)}), f32[16,2,32,256]{3,2,1,0:T(8,128)}, u32[]{:S(2)}, u32[]{:S(2)}) async-start(f32[16,2,32,256]{3,2,1,0:T(8,128)} %solve_inner.1), calls=%async_computation.2 | async-start | bytes 2097152 | tf_op jit(solution)/shard_map/all_to_all | solution.py:426
  12.6 16.5 %copy-start.5 = (bf16[2,128,256]{2,1,0:T(8,128)(2,1)S(1)}, bf16[2,128,256]{2,1,0:T(8,128)(2,1)}, u32[]{:S(2)}) copy-start(bf16[2,128,256]{2,1,0:T(8,128)(2,1)} %constant.29.clone.weights_ref) | copy-start | bytes 393220
  15.8 13.3 %collective-permute-start = (f32[32,4096]{1,0:T(8,128)S(1)}, f32[32,4096]{1,0:T(8,128)S(1)}, u32[]{:S(2)}, u32[]{:S(2)}) collective-permute-start(f32[32,4096]{1,0:T(8,128)S(1)} %get-tuple-element.8), channel_id=1, source_target_pairs={{0,16},{16,0},{1,17},{17,1},{2,18},{18,2},{3,19},{19,3},{4,20},{20... | collective-permute-start | bytes 1572872 | tf_op jit(solution)/shard_map/ppermute | solution.py:413
  29.1 13.6 %copy-start.3 = (f32[3,512,512]{2,1,0:T(8,128)S(1)}, f32[3,512,512]{2,1,0:T(8,128)}, u32[]{:S(2)}) copy-start(f32[3,512,512]{2,1,0:T(8,128)} %coupling_ref.1) | copy-start | bytes 9437188
  37.5 29.9 %all-to-all-start = ((f32[16,2,32,256]{3,2,1,0:T(8,128)}), f32[16,2,32,256]{3,2,1,0:T(8,128)}, u32[]{:S(2)}, u32[]{:S(2)}) async-start(f32[16,2,32,256]{3,2,1,0:T(8,128)} %solve_rim.1), calls=%async_computation | async-start | bytes 2097152 | tf_op jit(solution)/shard_map/all_to_all | solution.py:426
  54.4 2.1 %copy-start.1 = (bf16[3,512,1536]{2,1,0:T(8,128)(2,1)}, bf16[3,512,1536]{2,1,0:T(8,128)(2,1)S(1)}, u32[]{:S(2)}) copy-start(bf16[3,512,1536]{2,1,0:T(8,128)(2,1)S(1)} %split_mats.1.mats_ref) | copy-start | bytes 14155780
  67.5 29.8 %all-to-all-start.3 = ((f32[16,2,32,256]{3,2,1,0:T(8,128)}), f32[16,2,32,256]{3,2,1,0:T(8,128)S(1)}, u32[]{:S(2)}, u32[]{:S(2)}) async-start(f32[16,2,32,256]{3,2,1,0:T(8,128)} %repel.3), calls=%async_computation.3 | async-start | bytes 2097152 | tf_op jit(solution)/shard_map/all_to_all | solution.py:426
  72.4 2.3 %copy-start.2 = (bf16[3,512,1536]{2,1,0:T(8,128)(2,1)S(1)}, bf16[3,512,1536]{2,1,0:T(8,128)(2,1)}, u32[]{:S(2)}) copy-start(bf16[3,512,1536]{2,1,0:T(8,128)(2,1)} %copy-done.1) | copy-start | bytes 14155780
  97.3 29.8 %all-to-all-start.1 = ((f32[16,2,32,256]{3,2,1,0:T(8,128)}), f32[16,2,32,256]{3,2,1,0:T(8,128)S(1)}, u32[]{:S(2)}, u32[]{:S(2)}) async-start(f32[16,2,32,256]{3,2,1,0:T(8,128)} %repel.2), calls=%async_computation.1 | async-start | bytes 2097152 | tf_op jit(solution)/shard_map/all_to_all | solution.py:426

commit v3 on v2

--- a/solution.py
+++ b/solution.py
@@ -61,7 +61,7 @@
 
 def group_sums(value, weight):
     total = None
-    for _ in range(3):
+    for _ in range(2):
         part = value.astype(jnp.bfloat16)
         value = value - part.astype(jnp.float32)
         term = jnp.dot(part, weight, preferred_element_type=jnp.float32)

time: 129 us -> 129 us (level)
  no operation moved by 1% of the time
where the time goes in v3:
time: 129 us; the launch traced here: 128 us
  waiting for transfers between devices  64.6 us (50%)
  Pallas kernels  35.3 us (27%)
  starting transfers between devices  22.9 us (18%)
  local copies, waits for them, and re-layouts  4.63 us (4%)
    all_to_all x4, waiting for transfers between devices, exchange(): return lax.all_to_all(pieces, 'chan', 0, 0, tiled=True)  52.6 us
    all_to_all x4, starting transfers between devices, exchange(): return lax.all_to_all(pieces, 'chan', 0, 0, tiled=True)  21.7 us
    pallas_call x2, Pallas kernels, repel(): pl.pallas_call(repel_kernel, out_shape=jax.ShapeDtypeStruct(points.shape,...  20.1 us
    ppermute x1, waiting for transfers between devices, swap_halves(): lax.ppermute(part, axis, [(i, (i + devices // 2) % devices) for i in rang...  12 us
    pallas_call x2, Pallas kernels, solve_rows(): pl.pallas_call(functools.partial(solve_kernel, rim is not None, chan_size...  8.22 us
    unnamed x15, local copies, waits for them, and re-layouts  4.62 us
    pallas_call x1, Pallas kernels, outer_rows(): pl.pallas_call(functools.partial(outer_kernel, chan_size), out_shape=[jax...  3.15 us
  transfers between devices with their start and end apart: 5, of which 5 were waited for; matrix products, arithmetic and copies ran while one was open for 0% of the time, Pallas kernels for 23%

profile of v3, /device:TPU:9, one launch (start us, length us, event | category | flops | bytes accessed | tf_op | source)
XLA Modules:
  0.0 128.0 jit_solution(3841685406090146099)
XLA Ops:
  0.0 0.0 copy-start
  0.0 0.0 copy-start.6
  0.0 5.3 %solve_inner.1 = f32[16,2,32,256]{3,2,1,0:T(8,128)} custom-call(s32[3,512]{1,0:T(4,128)} %bitcast.4, f32[32,20,128]{2,1,0:T(8,128)} %constant.28.clone.table_ref, bf16[2,128,256]{2,1,0:T(8,128)(2,1)} %constant.29.clone.weights_ref, f32[32,4,4096]{2,1,0:T(4,128)} %refs_0_.1), custom_call_target="tpu_custom_call" | custom-call | flops 104857600 | bytes 8388608 | tf_op jit(solution)/shard_map/solve_inner/pallas_call | solution.py:246
  5.3 0.0 copy-start.4
  5.3 6.8 %all-to-all-start.2 = ((f32[16,2,32,256]{3,2,1,0:T(8,128)}), f32[16,2,32,256]{3,2,1,0:T(8,128)}, u32[]{:S(2)}, u32[]{:S(2)}) async-start(f32[16,2,32,256]{3,2,1,0:T(8,128)} %solve_inner.1), calls=%async_computation.2 | async-start | bytes 2097152 | tf_op jit(solution)/shard_map/all_to_all | solution.py:426
  12.1 0.0 copy-done
  12.1 0.0 copy-done.6
  12.1 0.0 copy-start.5
  12.1 3.1 %outer_rows.1 = (f32[32,4096]{1,0:T(8,128)S(1)}, f32[2,32,4096]{2,1,0:T(8,128)S(1)}) custom-call(s32[3,512]{1,0:T(4,128)S(1)} %bitcast.5, f32[32,4,4096]{2,1,0:T(4,128)S(1)} %copy-done), custom_call_target="tpu_custom_call" | custom-call | flops 4194304 | bytes 4194304 | tf_op jit(solution)/shard_map/outer_rows/pallas_call | solution.py:107
  15.2 1.3 collective-permute-start
  16.5 12.0 %collective-permute-done.refs_1_ = f32[32,4096]{1,0:T(8,128)S(1)} collective-permute-done((f32[32,4096]{1,0:T(8,128)S(1)}, f32[32,4096]{1,0:T(8,128)S(1)}, u32[]{:S(2)}, u32[]{:S(2)}) %collective-permute-start) | collective-permute-done | bytes 524320 | tf_op jit(solution)/shard_map/ppermute | solution.py:413
  28.6 0.0 copy-done.4
  28.6 0.0 copy-done.5
  28.6 0.0 copy-start.3
  28.6 2.9 %solve_rim.1 = f32[16,2,32,256]{3,2,1,0:T(8,128)} custom-call(s32[3,512]{1,0:T(4,128)S(1)} %bitcast.6, f32[32,20,128]{2,1,0:T(8,128)S(1)} %copy-done.4, bf16[2,128,256]{2,1,0:T(8,128)(2,1)S(1)} %copy-done.5, f32[2,32,4096]{2,1,0:T(8,128)S(1)} %get-tuple-element.7.refs_0_, f32[32,4096]{1,0:T(8,128)S(1)} %collective-permute-done.refs_1_), custom_call_target="tpu_custom_call" | custom-call | flops 52428800 | bytes 4194304 | tf_op jit(solution)/shard_map/solve_rim/pallas_call | solution.py:246
  31.5 5.5 %all-to-all-done.2.points_ref = f32[16,2,32,256]{3,2,1,0:T(8,128)} async-done(((f32[16,2,32,256]{3,2,1,0:T(8,128)}), f32[16,2,32,256]{3,2,1,0:T(8,128)}, u32[]{:S(2)}, u32[]{:S(2)}) %all-to-all-start.2) | async-done | bytes 1048608 | tf_op jit(solution)/shard_map/all_to_all | solution.py:426
  37.0 5.0 %all-to-all-start = ((f32[16,2,32,256]{3,2,1,0:T(8,128)}), f32[16,2,32,256]{3,2,1,0:T(8,128)}, u32[]{:S(2)}, u32[]{:S(2)}) async-start(f32[16,2,32,256]{3,2,1,0:T(8,128)} %solve_rim.1), calls=%async_computation | async-start | bytes 2097152 | tf_op jit(solution)/shard_map/all_to_all | solution.py:426
  42.0 0.1 copy.13.column_ref
  42.2 0.0 copy-done.3
  42.2 1.4 %split_mats.1.mats_ref = bf16[3,512,1536]{2,1,0:T(8,128)(2,1)S(1)} custom-call(f32[3,512,512]{2,1,0:T(8,128)S(1)} %copy-done.3, s32[512,1]{1,0:T(8,128)S(1)} %copy.13.column_ref, s32[1,512]{1,0:T(1,128)S(1)} %get-tuple-element.11.row_ref), custom_call_target="tpu_custom_call" | custom-call | flops 3145728 | bytes 7864320 | tf_op jit(solution)/shard_map/split_mats/pallas_call | solution.py:281
  43.6 0.1 maximum_divide_fusion
  43.8 10.0 %repel.3 = f32[16,2,32,256]{3,2,1,0:T(8,128)} custom-call(f32[16,2,32,256]{3,2,1,0:T(8,128)} %all-to-all-done.2.points_ref, bf16[3,512,1536]{2,1,0:T(8,128)(2,1)S(1)} %split_mats.1.mats_ref, f32[2,3,256]{2,1,0:T(4,128)S(1)} %get-tuple-element.9.factors_ref), custom_call_target="tpu_custom_call" | custom-call | flops 7247757312 | bytes 6815744 | tf_op jit(solution)/shard_map/repel/pallas_call | solution.py:339
  53.8 2.1 %copy-done.1 = bf16[3,512,1536]{2,1,0:T(8,128)(2,1)} copy-done((bf16[3,512,1536]{2,1,0:T(8,128)(2,1)}, bf16[3,512,1536]{2,1,0:T(8,128)(2,1)S(1)}, u32[]{:S(2)}) %copy-start.1) | copy-done | bytes 4718616
  55.9 11.0 %all-to-all-done.points_ref = f32[16,2,32,256]{3,2,1,0:T(8,128)} async-done(((f32[16,2,32,256]{3,2,1,0:T(8,128)}), f32[16,2,32,256]{3,2,1,0:T(8,128)}, u32[]{:S(2)}, u32[]{:S(2)}) %all-to-all-start) | async-done | bytes 1048608 | tf_op jit(solution)/shard_map/all_to_all | solution.py:426
  66.9 5.0 %all-to-all-start.3 = ((f32[16,2,32,256]{3,2,1,0:T(8,128)}), f32[16,2,32,256]{3,2,1,0:T(8,128)S(1)}, u32[]{:S(2)}, u32[]{:S(2)}) async-start(f32[16,2,32,256]{3,2,1,0:T(8,128)} %repel.3), calls=%async_computation.3 | async-start | bytes 2097152 | tf_op jit(solution)/shard_map/all_to_all | solution.py:426
  71.9 2.3 %copy-done.2 = bf16[3,512,1536]{2,1,0:T(8,128)(2,1)S(1)} copy-done((bf16[3,512,1536]{2,1,0:T(8,128)(2,1)S(1)}, bf16[3,512,1536]{2,1,0:T(8,128)(2,1)}, u32[]{:S(2)}) %copy-start.2) | copy-done | bytes 4718616
  74.2 10.0 %repel.2 = f32[16,2,32,256]{3,2,1,0:T(8,128)} custom-call(f32[16,2,32,256]{3,2,1,0:T(8,128)} %all-to-all-done.points_ref, bf16[3,512,1536]{2,1,0:T(8,128)(2,1)S(1)} %copy-done.2, f32[2,3,256]{2,1,0:T(4,128)S(1)} %get-tuple-element.10.factors_ref), custom_call_target="tpu_custom_call" | custom-call | flops 7247757312 | bytes 6815744 | tf_op jit(solution)/shard_map/repel/pallas_call | solution.py:339
  84.3 12.5 %all-to-all-done.3.piece_ref = f32[16,2,32,256]{3,2,1,0:T(8,128)S(1)} async-done(((f32[16,2,32,256]{3,2,1,0:T(8,128)}), f32[16,2,32,256]{3,2,1,0:T(8,128)S(1)}, u32[]{:S(2)}, u32[]{:S(2)}) %all-to-all-start.3) | async-done | bytes 1048608 | tf_op jit(solution)/shard_map/all_to_all | solution.py:426
  96.8 5.0 %all-to-all-start.1 = ((f32[16,2,32,256]{3,2,1,0:T(8,128)}), f32[16,2,32,256]{3,2,1,0:T(8,128)S(1)}, u32[]{:S(2)}, u32[]{:S(2)}) async-start(f32[16,2,32,256]{3,2,1,0:T(8,128)} %repel.2), calls=%async_computation.1 | async-start | bytes 2097152 | tf_op jit(solution)/shard_map/all_to_all | solution.py:426
  101.7 1.2 gather_first.1.refs_0_
  103.0 23.6 %all-to-all-done.1.piece_ref = f32[16,2,32,256]{3,2,1,0:T(8,128)S(1)} async-done(((f32[16,2,32,256]{3,2,1,0:T(8,128)}), f32[16,2,32,256]{3,2,1,0:T(8,128)S(1)}, u32[]{:S(2)}, u32[]{:S(2)}) %all-to-all-start.1) | async-done | bytes 1048608 | tf_op jit(solution)/shard_map/all_to_all | solution.py:426
  126.6 1.2 gather_last.1
  (6 shorter events, 0.0 us)
Async XLA Ops:
  0.0 12.1 %copy-start = (f32[32,4,4096]{2,1,0:T(4,128)S(1)}, f32[32,4,4096]{2,1,0:T(4,128)}, u32[]{:S(2)}) copy-start(f32[32,4,4096]{2,1,0:T(4,128)} %refs_0_.1) | copy-start | bytes 6291460
  0.0 12.1 %copy-start.6 = (s32[512,3]{0,1:T(4,128)S(1)}, s32[512,3]{0,1:T(4,128)}, u32[]{:S(2)}) copy-start(s32[512,3]{0,1:T(4,128)} %param.9) | copy-start | bytes 18436
  5.3 23.3 %copy-start.4 = (f32[32,20,128]{2,1,0:T(8,128)S(1)}, f32[32,20,128]{2,1,0:T(8,128)}, u32[]{:S(2)}) copy-start(f32[32,20,128]{2,1,0:T(8,128)} %constant.28.clone.table_ref) | copy-start | bytes 983044
  5.3 31.7 %all-to-all-start.2 = ((f32[16,2,32,256]{3,2,1,0:T(8,128)}), f32[16,2,32,256]{3,2,1,0:T(8,128)}, u32[]{:S(2)}, u32[]{:S(2)}) async-start(f32[16,2,32,256]{3,2,1,0:T(8,128)} %solve_inner.1), calls=%async_computation.2 | async-start | bytes 2097152 | tf_op jit(solution)/shard_map/all_to_all | solution.py:426
  12.1 16.5 %copy-start.5 = (bf16[2,128,256]{2,1,0:T(8,128)(2,1)S(1)}, bf16[2,128,256]{2,1,0:T(8,128)(2,1)}, u32[]{:S(2)}) copy-start(bf16[2,128,256]{2,1,0:T(8,128)(2,1)} %constant.29.clone.weights_ref) | copy-start | bytes 393220
  15.2 13.3 %collective-permute-start = (f32[32,4096]{1,0:T(8,128)S(1)}, f32[32,4096]{1,0:T(8,128)S(1)}, u32[]{:S(2)}, u32[]{:S(2)}) collective-permute-start(f32[32,4096]{1,0:T(8,128)S(1)} %get-tuple-element.8), channel_id=1, source_target_pairs={{0,16},{16,0},{1,17},{17,1},{2,18},{18,2},{3,19},{19,3},{4,20},{20... | collective-permute-start | bytes 1572872 | tf_op jit(solution)/shard_map/ppermute | solution.py:413
  28.6 13.6 %copy-start.3 = (f32[3,512,512]{2,1,0:T(8,128)S(1)}, f32[3,512,512]{2,1,0:T(8,128)}, u32[]{:S(2)}) copy-start(f32[3,512,512]{2,1,0:T(8,128)} %coupling_ref.1) | copy-start | bytes 9437188
  37.0 29.9 %all-to-all-start = ((f32[16,2,32,256]{3,2,1,0:T(8,128)}), f32[16,2,32,256]{3,2,1,0:T(8,128)}, u32[]{:S(2)}, u32[]{:S(2)}) async-start(f32[16,2,32,256]{3,2,1,0:T(8,128)} %solve_rim.1), calls=%async_computation | async-start | bytes 2097152 | tf_op jit(solution)/shard_map/all_to_all | solution.py:426
  53.8 2.1 %copy-start.1 = (bf16[3,512,1536]{2,1,0:T(8,128)(2,1)}, bf16[3,512,1536]{2,1,0:T(8,128)(2,1)S(1)}, u32[]{:S(2)}) copy-start(bf16[3,512,1536]{2,1,0:T(8,128)(2,1)S(1)} %split_mats.1.mats_ref) | copy-start | bytes 14155780
  66.9 29.8 %all-to-all-start.3 = ((f32[16,2,32,256]{3,2,1,0:T(8,128)}), f32[16,2,32,256]{3,2,1,0:T(8,128)S(1)}, u32[]{:S(2)}, u32[]{:S(2)}) async-start(f32[16,2,32,256]{3,2,1,0:T(8,128)} %repel.3), calls=%async_computation.3 | async-start | bytes 2097152 | tf_op jit(solution)/shard_map/all_to_all | solution.py:426
  71.9 2.3 %copy-start.2 = (bf16[3,512,1536]{2,1,0:T(8,128)(2,1)S(1)}, bf16[3,512,1536]{2,1,0:T(8,128)(2,1)}, u32[]{:S(2)}) copy-start(bf16[3,512,1536]{2,1,0:T(8,128)(2,1)} %copy-done.1) | copy-start | bytes 14155780
  96.8 29.8 %all-to-all-start.1 = ((f32[16,2,32,256]{3,2,1,0:T(8,128)}), f32[16,2,32,256]{3,2,1,0:T(8,128)S(1)}, u32[]{:S(2)}, u32[]{:S(2)}) async-start(f32[16,2,32,256]{3,2,1,0:T(8,128)} %repel.2), calls=%async_computation.1 | async-start | bytes 2097152 | tf_op jit(solution)/shard_map/all_to_all | solution.py:426

commit v4 on v3

--- a/solution.py
+++ b/solution.py
@@ -131,7 +131,6 @@
         rows_ref, in_sems = refs
     rad = lax.axis_index("rad")
     first = lax.axis_index("chan") * chan_size
-    which = channel_numbers(channels_ref, 0, first, nchan)
     side = step_tau / (2.0 * step_h * step_h)
     groups = in_sems.shape[0] if not with_rim else out_sems.shape[0]
     group = tiles // groups
@@ -159,6 +158,8 @@
             for copy in row_copies(step):
                 copy.start()
         rows = source_ref.shape[1]
+    which = channel_numbers(channels_ref, 0, first, nchan)
+    if not with_rim:
         scales = [row_scale(channels_ref, first, nchan, r, rad, rows) for r in range(1, rows - 1)]
 
     def fields_of(tile):

time: 129 us -> 128 us (level)
  no operation moved by 1% of the time
where the time goes in v4:
time: 128 us
  waiting for transfers between devices  64.6 us (50%)
  Pallas kernels  35.3 us (28%)
  starting transfers between devices  22.9 us (18%)
  local copies, waits for them, and re-layouts  4.63 us (4%)
    all_to_all x4, waiting for transfers between devices, exchange(): return lax.all_to_all(pieces, 'chan', 0, 0, tiled=True)  52.6 us
    all_to_all x4, starting transfers between devices, exchange(): return lax.all_to_all(pieces, 'chan', 0, 0, tiled=True)  21.7 us
    pallas_call x2, Pallas kernels, repel(): pl.pallas_call(repel_kernel, out_shape=jax.ShapeDtypeStruct(points.shape,...  20.1 us
    ppermute x1, waiting for transfers between devices, swap_halves(): lax.ppermute(part, axis, [(i, (i + devices // 2) % devices) for i in rang...  12 us
    pallas_call x2, Pallas kernels, solve_rows(): pl.pallas_call(functools.partial(solve_kernel, rim is not None, chan_size...  8.16 us
    unnamed x15, local copies, waits for them, and re-layouts  4.62 us
    pallas_call x1, Pallas kernels, outer_rows(): pl.pallas_call(functools.partial(outer_kernel, chan_size), out_shape=[jax...  3.15 us
  transfers between devices with their start and end apart: 5, of which 5 were waited for; matrix products, arithmetic and copies ran while one was open for 0% of the time, Pallas kernels for 23%

profile of v4, /device:TPU:9, one launch (start us, length us, event | category | flops | bytes accessed | tf_op | source)
XLA Modules:
  0.0 127.9 jit_solution(1604220475539572462)
XLA Ops:
  0.0 0.0 copy-start
  0.0 5.2 %solve_inner.1 = f32[16,2,32,256]{3,2,1,0:T(8,128)} custom-call(s32[3,512]{1,0:T(4,128)} %bitcast.4, f32[32,20,128]{2,1,0:T(8,128)} %constant.28.clone.table_ref, bf16[2,128,256]{2,1,0:T(8,128)(2,1)} %constant.29.clone.weights_ref, f32[32,4,4096]{2,1,0:T(4,128)} %refs_0_.1), custom_call_target="tpu_custom_call" | custom-call | flops 104857600 | bytes 8388608 | tf_op jit(solution)/shard_map/solve_inner/pallas_call | solution.py:247
  5.2 0.0 copy-start.4
  5.3 6.8 %all-to-all-start.2 = ((f32[16,2,32,256]{3,2,1,0:T(8,128)}), f32[16,2,32,256]{3,2,1,0:T(8,128)}, u32[]{:S(2)}, u32[]{:S(2)}) async-start(f32[16,2,32,256]{3,2,1,0:T(8,128)} %solve_inner.1), calls=%async_computation.2 | async-start | bytes 2097152 | tf_op jit(solution)/shard_map/all_to_all | solution.py:427
  12.0 0.0 copy-done
  12.0 0.0 copy-done.6
  12.0 0.0 copy-start.5
  12.0 3.1 %outer_rows.1 = (f32[32,4096]{1,0:T(8,128)S(1)}, f32[2,32,4096]{2,1,0:T(8,128)S(1)}) custom-call(s32[3,512]{1,0:T(4,128)S(1)} %bitcast.5, f32[32,4,4096]{2,1,0:T(4,128)S(1)} %copy-done), custom_call_target="tpu_custom_call" | custom-call | flops 4194304 | bytes 4194304 | tf_op jit(solution)/shard_map/outer_rows/pallas_call | solution.py:107
  15.2 1.3 collective-permute-start
  16.5 12.0 %collective-permute-done.refs_1_ = f32[32,4096]{1,0:T(8,128)S(1)} collective-permute-done((f32[32,4096]{1,0:T(8,128)S(1)}, f32[32,4096]{1,0:T(8,128)S(1)}, u32[]{:S(2)}, u32[]{:S(2)}) %collective-permute-start) | collective-permute-done | bytes 524320 | tf_op jit(solution)/shard_map/ppermute | solution.py:414
  28.5 0.0 copy-done.4
  28.5 0.0 copy-done.5
  28.5 0.0 copy-start.3
  28.5 2.9 %solve_rim.1 = f32[16,2,32,256]{3,2,1,0:T(8,128)} custom-call(s32[3,512]{1,0:T(4,128)S(1)} %bitcast.6, f32[32,20,128]{2,1,0:T(8,128)S(1)} %copy-done.4, bf16[2,128,256]{2,1,0:T(8,128)(2,1)S(1)} %copy-done.5, f32[2,32,4096]{2,1,0:T(8,128)S(1)} %get-tuple-element.7.refs_0_, f32[32,4096]{1,0:T(8,128)S(1)} %collective-permute-done.refs_1_), custom_call_target="tpu_custom_call" | custom-call | flops 52428800 | bytes 4194304 | tf_op jit(solution)/shard_map/solve_rim/pallas_call | solution.py:247
  31.5 5.5 %all-to-all-done.2.points_ref = f32[16,2,32,256]{3,2,1,0:T(8,128)} async-done(((f32[16,2,32,256]{3,2,1,0:T(8,128)}), f32[16,2,32,256]{3,2,1,0:T(8,128)}, u32[]{:S(2)}, u32[]{:S(2)}) %all-to-all-start.2) | async-done | bytes 1048608 | tf_op jit(solution)/shard_map/all_to_all | solution.py:427
  37.0 5.0 %all-to-all-start = ((f32[16,2,32,256]{3,2,1,0:T(8,128)}), f32[16,2,32,256]{3,2,1,0:T(8,128)}, u32[]{:S(2)}, u32[]{:S(2)}) async-start(f32[16,2,32,256]{3,2,1,0:T(8,128)} %solve_rim.1), calls=%async_computation | async-start | bytes 2097152 | tf_op jit(solution)/shard_map/all_to_all | solution.py:427
  41.9 0.1 copy.13.column_ref
  42.1 0.0 copy-done.3
  42.1 1.4 %split_mats.1.mats_ref = bf16[3,512,1536]{2,1,0:T(8,128)(2,1)S(1)} custom-call(f32[3,512,512]{2,1,0:T(8,128)S(1)} %copy-done.3, s32[512,1]{1,0:T(8,128)S(1)} %copy.13.column_ref, s32[1,512]{1,0:T(1,128)S(1)} %get-tuple-element.11.row_ref), custom_call_target="tpu_custom_call" | custom-call | flops 3145728 | bytes 7864320 | tf_op jit(solution)/shard_map/split_mats/pallas_call | solution.py:282
  43.6 0.1 maximum_divide_fusion
  43.7 10.0 %repel.3 = f32[16,2,32,256]{3,2,1,0:T(8,128)} custom-call(f32[16,2,32,256]{3,2,1,0:T(8,128)} %all-to-all-done.2.points_ref, bf16[3,512,1536]{2,1,0:T(8,128)(2,1)S(1)} %split_mats.1.mats_ref, f32[2,3,256]{2,1,0:T(4,128)S(1)} %get-tuple-element.9.factors_ref), custom_call_target="tpu_custom_call" | custom-call | flops 7247757312 | bytes 6815744 | tf_op jit(solution)/shard_map/repel/pallas_call | solution.py:340
  53.7 0.0 copy-start.1
  53.8 2.1 %copy-done.1 = bf16[3,512,1536]{2,1,0:T(8,128)(2,1)} copy-done((bf16[3,512,1536]{2,1,0:T(8,128)(2,1)}, bf16[3,512,1536]{2,1,0:T(8,128)(2,1)S(1)}, u32[]{:S(2)}) %copy-start.1) | copy-done | bytes 4718616
  55.9 11.0 %all-to-all-done.points_ref = f32[16,2,32,256]{3,2,1,0:T(8,128)} async-done(((f32[16,2,32,256]{3,2,1,0:T(8,128)}), f32[16,2,32,256]{3,2,1,0:T(8,128)}, u32[]{:S(2)}, u32[]{:S(2)}) %all-to-all-start) | async-done | bytes 1048608 | tf_op jit(solution)/shard_map/all_to_all | solution.py:427
  66.9 5.0 %all-to-all-start.3 = ((f32[16,2,32,256]{3,2,1,0:T(8,128)}), f32[16,2,32,256]{3,2,1,0:T(8,128)S(1)}, u32[]{:S(2)}, u32[]{:S(2)}) async-start(f32[16,2,32,256]{3,2,1,0:T(8,128)} %repel.3), calls=%async_computation.3 | async-start | bytes 2097152 | tf_op jit(solution)/shard_map/all_to_all | solution.py:427
  71.9 2.3 %copy-done.2 = bf16[3,512,1536]{2,1,0:T(8,128)(2,1)S(1)} copy-done((bf16[3,512,1536]{2,1,0:T(8,128)(2,1)S(1)}, bf16[3,512,1536]{2,1,0:T(8,128)(2,1)}, u32[]{:S(2)}) %copy-start.2) | copy-done | bytes 4718616
  74.2 10.0 %repel.2 = f32[16,2,32,256]{3,2,1,0:T(8,128)} custom-call(f32[16,2,32,256]{3,2,1,0:T(8,128)} %all-to-all-done.points_ref, bf16[3,512,1536]{2,1,0:T(8,128)(2,1)S(1)} %copy-done.2, f32[2,3,256]{2,1,0:T(4,128)S(1)} %get-tuple-element.10.factors_ref), custom_call_target="tpu_custom_call" | custom-call | flops 7247757312 | bytes 6815744 | tf_op jit(solution)/shard_map/repel/pallas_call | solution.py:340
  84.2 12.5 %all-to-all-done.3.piece_ref = f32[16,2,32,256]{3,2,1,0:T(8,128)S(1)} async-done(((f32[16,2,32,256]{3,2,1,0:T(8,128)}), f32[16,2,32,256]{3,2,1,0:T(8,128)S(1)}, u32[]{:S(2)}, u32[]{:S(2)}) %all-to-all-start.3) | async-done | bytes 1048608 | tf_op jit(solution)/shard_map/all_to_all | solution.py:427
  96.7 5.0 %all-to-all-start.1 = ((f32[16,2,32,256]{3,2,1,0:T(8,128)}), f32[16,2,32,256]{3,2,1,0:T(8,128)S(1)}, u32[]{:S(2)}, u32[]{:S(2)}) async-start(f32[16,2,32,256]{3,2,1,0:T(8,128)} %repel.2), calls=%async_computation.1 | async-start | bytes 2097152 | tf_op jit(solution)/shard_map/all_to_all | solution.py:427
  101.7 1.2 gather_first.1.refs_0_
  102.9 23.6 %all-to-all-done.1.piece_ref = f32[16,2,32,256]{3,2,1,0:T(8,128)S(1)} async-done(((f32[16,2,32,256]{3,2,1,0:T(8,128)}), f32[16,2,32,256]{3,2,1,0:T(8,128)S(1)}, u32[]{:S(2)}, u32[]{:S(2)}) %all-to-all-start.1) | async-done | bytes 1048608 | tf_op jit(solution)/shard_map/all_to_all | solution.py:427
  126.5 1.2 gather_last.1
  (6 shorter events, 0.0 us)
Async XLA Ops:
  0.0 12.0 %copy-start = (f32[32,4,4096]{2,1,0:T(4,128)S(1)}, f32[32,4,4096]{2,1,0:T(4,128)}, u32[]{:S(2)}) copy-start(f32[32,4,4096]{2,1,0:T(4,128)} %refs_0_.1) | copy-start | bytes 6291460
  0.0 12.0 %copy-start.6 = (s32[512,3]{0,1:T(4,128)S(1)}, s32[512,3]{0,1:T(4,128)}, u32[]{:S(2)}) copy-start(s32[512,3]{0,1:T(4,128)} %param.9) | copy-start | bytes 18436
  5.2 23.3 %copy-start.4 = (f32[32,20,128]{2,1,0:T(8,128)S(1)}, f32[32,20,128]{2,1,0:T(8,128)}, u32[]{:S(2)}) copy-start(f32[32,20,128]{2,1,0:T(8,128)} %constant.28.clone.table_ref) | copy-start | bytes 983044
  5.3 31.7 %all-to-all-start.2 = ((f32[16,2,32,256]{3,2,1,0:T(8,128)}), f32[16,2,32,256]{3,2,1,0:T(8,128)}, u32[]{:S(2)}, u32[]{:S(2)}) async-start(f32[16,2,32,256]{3,2,1,0:T(8,128)} %solve_inner.1), calls=%async_computation.2 | async-start | bytes 2097152 | tf_op jit(solution)/shard_map/all_to_all | solution.py:427
  12.0 16.5 %copy-start.5 = (bf16[2,128,256]{2,1,0:T(8,128)(2,1)S(1)}, bf16[2,128,256]{2,1,0:T(8,128)(2,1)}, u32[]{:S(2)}) copy-start(bf16[2,128,256]{2,1,0:T(8,128)(2,1)} %constant.29.clone.weights_ref) | copy-start | bytes 393220
  15.2 13.3 %collective-permute-start = (f32[32,4096]{1,0:T(8,128)S(1)}, f32[32,4096]{1,0:T(8,128)S(1)}, u32[]{:S(2)}, u32[]{:S(2)}) collective-permute-start(f32[32,4096]{1,0:T(8,128)S(1)} %get-tuple-element.8), channel_id=1, source_target_pairs={{0,16},{16,0},{1,17},{17,1},{2,18},{18,2},{3,19},{19,3},{4,20},{20... | collective-permute-start | bytes 1572872 | tf_op jit(solution)/shard_map/ppermute | solution.py:414
  28.5 13.6 %copy-start.3 = (f32[3,512,512]{2,1,0:T(8,128)S(1)}, f32[3,512,512]{2,1,0:T(8,128)}, u32[]{:S(2)}) copy-start(f32[3,512,512]{2,1,0:T(8,128)} %coupling_ref.1) | copy-start | bytes 9437188
  37.0 29.9 %all-to-all-start = ((f32[16,2,32,256]{3,2,1,0:T(8,128)}), f32[16,2,32,256]{3,2,1,0:T(8,128)}, u32[]{:S(2)}, u32[]{:S(2)}) async-start(f32[16,2,32,256]{3,2,1,0:T(8,128)} %solve_rim.1), calls=%async_computation | async-start | bytes 2097152 | tf_op jit(solution)/shard_map/all_to_all | solution.py:427
  53.7 2.1 %copy-start.1 = (bf16[3,512,1536]{2,1,0:T(8,128)(2,1)}, bf16[3,512,1536]{2,1,0:T(8,128)(2,1)S(1)}, u32[]{:S(2)}) copy-start(bf16[3,512,1536]{2,1,0:T(8,128)(2,1)S(1)} %split_mats.1.mats_ref) | copy-start | bytes 14155780
  66.9 29.8 %all-to-all-start.3 = ((f32[16,2,32,256]{3,2,1,0:T(8,128)}), f32[16,2,32,256]{3,2,1,0:T(8,128)S(1)}, u32[]{:S(2)}, u32[]{:S(2)}) async-start(f32[16,2,32,256]{3,2,1,0:T(8,128)} %repel.3), calls=%async_computation.3 | async-start | bytes 2097152 | tf_op jit(solution)/shard_map/all_to_all | solution.py:427
  71.8 2.3 %copy-start.2 = (bf16[3,512,1536]{2,1,0:T(8,128)(2,1)S(1)}, bf16[3,512,1536]{2,1,0:T(8,128)(2,1)}, u32[]{:S(2)}) copy-start(bf16[3,512,1536]{2,1,0:T(8,128)(2,1)} %copy-done.1) | copy-start | bytes 14155780
  96.7 29.8 %all-to-all-start.1 = ((f32[16,2,32,256]{3,2,1,0:T(8,128)}), f32[16,2,32,256]{3,2,1,0:T(8,128)S(1)}, u32[]{:S(2)}, u32[]{:S(2)}) async-start(f32[16,2,32,256]{3,2,1,0:T(8,128)} %repel.2), calls=%async_computation.1 | async-start | bytes 2097152 | tf_op jit(solution)/shard_map/all_to_all | solution.py:427

commit v5 on v3

--- a/solution.py
+++ b/solution.py
@@ -230,7 +230,7 @@
         operands.append(rim)
     vmem = pl.BlockSpec(memory_space=pltpu.VMEM)
     anywhere = pl.BlockSpec(memory_space=pl.ANY)
-    groups = 4
+    groups = 2
     scratch = [
         pltpu.VMEM(piece, jnp.float32),
         pltpu.VMEM((count, tiles, nchan, lanes), jnp.float32),

time: 129 us -> 128 us (level)
  no operation moved by 1% of the time
where the time goes in v5:
time: 128 us
  waiting for transfers between devices  64.4 us (50%)
  Pallas kernels  35.4 us (28%)
  starting transfers between devices  22.9 us (18%)
  local copies, waits for them, and re-layouts  4.63 us (4%)
    all_to_all x4, waiting for transfers between devices, exchange(): return lax.all_to_all(pieces, 'chan', 0, 0, tiled=True)  52.4 us
    all_to_all x4, starting transfers between devices, exchange(): return lax.all_to_all(pieces, 'chan', 0, 0, tiled=True)  21.7 us
    pallas_call x2, Pallas kernels, repel(): pl.pallas_call(repel_kernel, out_shape=jax.ShapeDtypeStruct(points.shape,...  20.1 us
    ppermute x1, waiting for transfers between devices, swap_halves(): lax.ppermute(part, axis, [(i, (i + devices // 2) % devices) for i in rang...  12 us
    pallas_call x2, Pallas kernels, solve_rows(): pl.pallas_call(functools.partial(solve_kernel, rim is not None, chan_size...  8.28 us
    unnamed x15, local copies, waits for them, and re-layouts  4.62 us
    pallas_call x1, Pallas kernels, outer_rows(): pl.pallas_call(functools.partial(outer_kernel, chan_size), out_shape=[jax...  3.15 us
  transfers between devices with their start and end apart: 5, of which 5 were waited for; matrix products, arithmetic and copies ran while one was open for 0% of the time, Pallas kernels for 23%

profile of v5, /device:TPU:9, one launch (start us, length us, event | category | flops | bytes accessed | tf_op | source)
XLA Modules:
  0.0 127.8 jit_solution(13699352676951500577)
XLA Ops:
  0.0 0.0 copy-start
  0.0 0.0 copy-start.6
  0.0 5.1 %solve_inner.1 = f32[16,2,32,256]{3,2,1,0:T(8,128)} custom-call(s32[3,512]{1,0:T(4,128)} %bitcast.4, f32[32,20,128]{2,1,0:T(8,128)} %constant.28.clone.table_ref, bf16[2,128,256]{2,1,0:T(8,128)(2,1)} %constant.29.clone.weights_ref, f32[32,4,4096]{2,1,0:T(4,128)} %refs_0_.1), custom_call_target="tpu_custom_call" | custom-call | flops 104857600 | bytes 8388608 | tf_op jit(solution)/shard_map/solve_inner/pallas_call | solution.py:246
  5.1 0.0 copy-start.4
  5.2 6.8 %all-to-all-start.2 = ((f32[16,2,32,256]{3,2,1,0:T(8,128)}), f32[16,2,32,256]{3,2,1,0:T(8,128)}, u32[]{:S(2)}, u32[]{:S(2)}) async-start(f32[16,2,32,256]{3,2,1,0:T(8,128)} %solve_inner.1), calls=%async_computation.2 | async-start | bytes 2097152 | tf_op jit(solution)/shard_map/all_to_all | solution.py:426
  11.9 0.0 copy-done
  11.9 0.0 copy-done.6
  11.9 0.0 copy-start.5
  11.9 3.1 %outer_rows.1 = (f32[32,4096]{1,0:T(8,128)S(1)}, f32[2,32,4096]{2,1,0:T(8,128)S(1)}) custom-call(s32[3,512]{1,0:T(4,128)S(1)} %bitcast.5, f32[32,4,4096]{2,1,0:T(4,128)S(1)} %copy-done), custom_call_target="tpu_custom_call" | custom-call | flops 4194304 | bytes 4194304 | tf_op jit(solution)/shard_map/outer_rows/pallas_call | solution.py:107
  15.1 1.3 collective-permute-start
  16.4 12.0 %collective-permute-done.refs_1_ = f32[32,4096]{1,0:T(8,128)S(1)} collective-permute-done((f32[32,4096]{1,0:T(8,128)S(1)}, f32[32,4096]{1,0:T(8,128)S(1)}, u32[]{:S(2)}, u32[]{:S(2)}) %collective-permute-start) | collective-permute-done | bytes 524320 | tf_op jit(solution)/shard_map/ppermute | solution.py:413
  28.4 0.0 copy-done.4
  28.4 0.0 copy-done.5
  28.4 0.0 copy-start.3
  28.4 3.1 %solve_rim.1 = f32[16,2,32,256]{3,2,1,0:T(8,128)} custom-call(s32[3,512]{1,0:T(4,128)S(1)} %bitcast.6, f32[32,20,128]{2,1,0:T(8,128)S(1)} %copy-done.4, bf16[2,128,256]{2,1,0:T(8,128)(2,1)S(1)} %copy-done.5, f32[2,32,4096]{2,1,0:T(8,128)S(1)} %get-tuple-element.7.refs_0_, f32[32,4096]{1,0:T(8,128)S(1)} %collective-permute-done.refs_1_), custom_call_target="tpu_custom_call" | custom-call | flops 52428800 | bytes 4194304 | tf_op jit(solution)/shard_map/solve_rim/pallas_call | solution.py:246
  31.6 5.3 %all-to-all-done.2.points_ref = f32[16,2,32,256]{3,2,1,0:T(8,128)} async-done(((f32[16,2,32,256]{3,2,1,0:T(8,128)}), f32[16,2,32,256]{3,2,1,0:T(8,128)}, u32[]{:S(2)}, u32[]{:S(2)}) %all-to-all-start.2) | async-done | bytes 1048608 | tf_op jit(solution)/shard_map/all_to_all | solution.py:426
  36.9 5.0 %all-to-all-start = ((f32[16,2,32,256]{3,2,1,0:T(8,128)}), f32[16,2,32,256]{3,2,1,0:T(8,128)}, u32[]{:S(2)}, u32[]{:S(2)}) async-start(f32[16,2,32,256]{3,2,1,0:T(8,128)} %solve_rim.1), calls=%async_computation | async-start | bytes 2097152 | tf_op jit(solution)/shard_map/all_to_all | solution.py:426
  41.8 0.1 copy.13.column_ref
  42.0 0.0 copy-done.3
  42.0 1.4 %split_mats.1.mats_ref = bf16[3,512,1536]{2,1,0:T(8,128)(2,1)S(1)} custom-call(f32[3,512,512]{2,1,0:T(8,128)S(1)} %copy-done.3, s32[512,1]{1,0:T(8,128)S(1)} %copy.13.column_ref, s32[1,512]{1,0:T(1,128)S(1)} %get-tuple-element.11.row_ref), custom_call_target="tpu_custom_call" | custom-call | flops 3145728 | bytes 7864320 | tf_op jit(solution)/shard_map/split_mats/pallas_call | solution.py:281
  43.5 0.1 maximum_divide_fusion
  43.6 10.1 %repel.3 = f32[16,2,32,256]{3,2,1,0:T(8,128)} custom-call(f32[16,2,32,256]{3,2,1,0:T(8,128)} %all-to-all-done.2.points_ref, bf16[3,512,1536]{2,1,0:T(8,128)(2,1)S(1)} %split_mats.1.mats_ref, f32[2,3,256]{2,1,0:T(4,128)S(1)} %get-tuple-element.9.factors_ref), custom_call_target="tpu_custom_call" | custom-call | flops 7247757312 | bytes 6815744 | tf_op jit(solution)/shard_map/repel/pallas_call | solution.py:339
  53.7 2.1 %copy-done.1 = bf16[3,512,1536]{2,1,0:T(8,128)(2,1)} copy-done((bf16[3,512,1536]{2,1,0:T(8,128)(2,1)}, bf16[3,512,1536]{2,1,0:T(8,128)(2,1)S(1)}, u32[]{:S(2)}) %copy-start.1) | copy-done | bytes 4718616
  55.8 11.0 %all-to-all-done.points_ref = f32[16,2,32,256]{3,2,1,0:T(8,128)} async-done(((f32[16,2,32,256]{3,2,1,0:T(8,128)}), f32[16,2,32,256]{3,2,1,0:T(8,128)}, u32[]{:S(2)}, u32[]{:S(2)}) %all-to-all-start) | async-done | bytes 1048608 | tf_op jit(solution)/shard_map/all_to_all | solution.py:426
  66.8 5.0 %all-to-all-start.3 = ((f32[16,2,32,256]{3,2,1,0:T(8,128)}), f32[16,2,32,256]{3,2,1,0:T(8,128)S(1)}, u32[]{:S(2)}, u32[]{:S(2)}) async-start(f32[16,2,32,256]{3,2,1,0:T(8,128)} %repel.3), calls=%async_computation.3 | async-start | bytes 2097152 | tf_op jit(solution)/shard_map/all_to_all | solution.py:426
  71.8 2.3 %copy-done.2 = bf16[3,512,1536]{2,1,0:T(8,128)(2,1)S(1)} copy-done((bf16[3,512,1536]{2,1,0:T(8,128)(2,1)S(1)}, bf16[3,512,1536]{2,1,0:T(8,128)(2,1)}, u32[]{:S(2)}) %copy-start.2) | copy-done | bytes 4718616
  74.1 10.0 %repel.2 = f32[16,2,32,256]{3,2,1,0:T(8,128)} custom-call(f32[16,2,32,256]{3,2,1,0:T(8,128)} %all-to-all-done.points_ref, bf16[3,512,1536]{2,1,0:T(8,128)(2,1)S(1)} %copy-done.2, f32[2,3,256]{2,1,0:T(4,128)S(1)} %get-tuple-element.10.factors_ref), custom_call_target="tpu_custom_call" | custom-call | flops 7247757312 | bytes 6815744 | tf_op jit(solution)/shard_map/repel/pallas_call | solution.py:339
  84.1 12.5 %all-to-all-done.3.piece_ref = f32[16,2,32,256]{3,2,1,0:T(8,128)S(1)} async-done(((f32[16,2,32,256]{3,2,1,0:T(8,128)}), f32[16,2,32,256]{3,2,1,0:T(8,128)S(1)}, u32[]{:S(2)}, u32[]{:S(2)}) %all-to-all-start.3) | async-done | bytes 1048608 | tf_op jit(solution)/shard_map/all_to_all | solution.py:426
  96.6 5.0 %all-to-all-start.1 = ((f32[16,2,32,256]{3,2,1,0:T(8,128)}), f32[16,2,32,256]{3,2,1,0:T(8,128)S(1)}, u32[]{:S(2)}, u32[]{:S(2)}) async-start(f32[16,2,32,256]{3,2,1,0:T(8,128)} %repel.2), calls=%async_computation.1 | async-start | bytes 2097152 | tf_op jit(solution)/shard_map/all_to_all | solution.py:426
  101.6 1.2 gather_first.1.refs_0_
  102.8 23.6 %all-to-all-done.1.piece_ref = f32[16,2,32,256]{3,2,1,0:T(8,128)S(1)} async-done(((f32[16,2,32,256]{3,2,1,0:T(8,128)}), f32[16,2,32,256]{3,2,1,0:T(8,128)S(1)}, u32[]{:S(2)}, u32[]{:S(2)}) %all-to-all-start.1) | async-done | bytes 1048608 | tf_op jit(solution)/shard_map/all_to_all | solution.py:426
  126.4 1.2 gather_last.1
  (6 shorter events, 0.0 us)
Async XLA Ops:
  0.0 11.9 %copy-start = (f32[32,4,4096]{2,1,0:T(4,128)S(1)}, f32[32,4,4096]{2,1,0:T(4,128)}, u32[]{:S(2)}) copy-start(f32[32,4,4096]{2,1,0:T(4,128)} %refs_0_.1) | copy-start | bytes 6291460
  0.0 11.9 %copy-start.6 = (s32[512,3]{0,1:T(4,128)S(1)}, s32[512,3]{0,1:T(4,128)}, u32[]{:S(2)}) copy-start(s32[512,3]{0,1:T(4,128)} %param.9) | copy-start | bytes 18436
  5.1 23.3 %copy-start.4 = (f32[32,20,128]{2,1,0:T(8,128)S(1)}, f32[32,20,128]{2,1,0:T(8,128)}, u32[]{:S(2)}) copy-start(f32[32,20,128]{2,1,0:T(8,128)} %constant.28.clone.table_ref) | copy-start | bytes 983044
  5.2 31.7 %all-to-all-start.2 = ((f32[16,2,32,256]{3,2,1,0:T(8,128)}), f32[16,2,32,256]{3,2,1,0:T(8,128)}, u32[]{:S(2)}, u32[]{:S(2)}) async-start(f32[16,2,32,256]{3,2,1,0:T(8,128)} %solve_inner.1), calls=%async_computation.2 | async-start | bytes 2097152 | tf_op jit(solution)/shard_map/all_to_all | solution.py:426
  11.9 16.5 %copy-start.5 = (bf16[2,128,256]{2,1,0:T(8,128)(2,1)S(1)}, bf16[2,128,256]{2,1,0:T(8,128)(2,1)}, u32[]{:S(2)}) copy-start(bf16[2,128,256]{2,1,0:T(8,128)(2,1)} %constant.29.clone.weights_ref) | copy-start | bytes 393220
  15.1 13.3 %collective-permute-start = (f32[32,4096]{1,0:T(8,128)S(1)}, f32[32,4096]{1,0:T(8,128)S(1)}, u32[]{:S(2)}, u32[]{:S(2)}) collective-permute-start(f32[32,4096]{1,0:T(8,128)S(1)} %get-tuple-element.8), channel_id=1, source_target_pairs={{0,16},{16,0},{1,17},{17,1},{2,18},{18,2},{3,19},{19,3},{4,20},{20... | collective-permute-start | bytes 1572872 | tf_op jit(solution)/shard_map/ppermute | solution.py:413
  28.4 13.6 %copy-start.3 = (f32[3,512,512]{2,1,0:T(8,128)S(1)}, f32[3,512,512]{2,1,0:T(8,128)}, u32[]{:S(2)}) copy-start(f32[3,512,512]{2,1,0:T(8,128)} %coupling_ref.1) | copy-start | bytes 9437188
  36.9 29.9 %all-to-all-start = ((f32[16,2,32,256]{3,2,1,0:T(8,128)}), f32[16,2,32,256]{3,2,1,0:T(8,128)}, u32[]{:S(2)}, u32[]{:S(2)}) async-start(f32[16,2,32,256]{3,2,1,0:T(8,128)} %solve_rim.1), calls=%async_computation | async-start | bytes 2097152 | tf_op jit(solution)/shard_map/all_to_all | solution.py:426
  53.7 2.1 %copy-start.1 = (bf16[3,512,1536]{2,1,0:T(8,128)(2,1)}, bf16[3,512,1536]{2,1,0:T(8,128)(2,1)S(1)}, u32[]{:S(2)}) copy-start(bf16[3,512,1536]{2,1,0:T(8,128)(2,1)S(1)} %split_mats.1.mats_ref) | copy-start | bytes 14155780
  66.8 29.8 %all-to-all-start.3 = ((f32[16,2,32,256]{3,2,1,0:T(8,128)}), f32[16,2,32,256]{3,2,1,0:T(8,128)S(1)}, u32[]{:S(2)}, u32[]{:S(2)}) async-start(f32[16,2,32,256]{3,2,1,0:T(8,128)} %repel.3), calls=%async_computation.3 | async-start | bytes 2097152 | tf_op jit(solution)/shard_map/all_to_all | solution.py:426
  71.8 2.3 %copy-start.2 = (bf16[3,512,1536]{2,1,0:T(8,128)(2,1)S(1)}, bf16[3,512,1536]{2,1,0:T(8,128)(2,1)}, u32[]{:S(2)}) copy-start(bf16[3,512,1536]{2,1,0:T(8,128)(2,1)} %copy-done.1) | copy-start | bytes 14155780
  96.6 29.8 %all-to-all-start.1 = ((f32[16,2,32,256]{3,2,1,0:T(8,128)}), f32[16,2,32,256]{3,2,1,0:T(8,128)S(1)}, u32[]{:S(2)}, u32[]{:S(2)}) async-start(f32[16,2,32,256]{3,2,1,0:T(8,128)} %repel.2), calls=%async_computation.1 | async-start | bytes 2097152 | tf_op jit(solution)/shard_map/all_to_all | solution.py:426
